TPU v7x, 32 devices: a whole 2x2x4 slice. The times are simulated.
32 devices in a mesh: parts: 2 (over y), blk: 4 (over z), users: 2 (over x), sub: 2 (over core).
Axes of the slice: x: 2, y: 2, z: 4, core: 2. Of those that a mesh axis runs over, the one named last changes fastest.
Arguments:
- history: bfloat16 [64, 64, 256], P(('parts', 'blk'), 'users'), parts along dimension 0, may hold values from -400 to 400
- lengths: int32 [64], P(('parts', 'blk')), parts along dimension 0, may hold values from 1 to 64
- item_rows: bfloat16 [12288, 512], P(('parts', 'blk', 'users', 'sub')), parts along dimension 0, may hold values from -6 to 6
- w_query: bfloat16 [512, 256], replicated, may hold values from -0.25 to 0.25
- w_item: bfloat16 [512, 256], replicated, may hold values from -0.25 to 0.25
- w_key: bfloat16 [256, 256], replicated, may hold values from -0.375 to 0.375
- w_value: bfloat16 [256, 256], replicated, may hold values from -0.375 to 0.375
- w_pooled: bfloat16 [256, 128], replicated, may hold values from -0.25 to 0.25
- w_joint: bfloat16 [256, 128], replicated, may hold values from -0.25 to 0.25
- bias_hidden: float32 [128], replicated, may hold values from -3 to 3
- w_task: bfloat16 [128, 8], replicated, may hold values from -0.5 to 0.5
- bias_task: float32 [8], replicated, may hold values from -3 to 3
Outputs:
- logits: float32 [64, 9, 8, 1536], P(('parts', 'blk'), None, None, ('users', 'sub')), parts along dimension 0
There are 2 independent parts, one for each index of `parts`. A program takes and returns all parts, laid end to end along the dimension named above; an argument that names none is the same for every part. Nothing has to cross between parts.
All inputs are finite; a program needn't handle non-finite values.
Results may differ from a plain program's by a relative error of at most 0.011.
Values may be sent and summed in bfloat16 or wider, within the bound.
A program may use at most 64 MiB of HBM per device.

v0:
```python
import math

import jax
import jax.numpy as jnp
from jax import lax
from jax.sharding import PartitionSpec as P

DH = 256
REACH = 4
WIN = 9


def shifted(block, axis, distance):
    devices = range(lax.axis_size(axis))
    route = [((i - distance) % len(devices), i) for i in devices]
    return lax.ppermute(block, axis, route)


def project(item_rows, w_query, w_item, w_joint, bias_hidden):
    queries = jnp.dot(item_rows, w_query, preferred_element_type=jnp.float32).astype(jnp.bfloat16)
    joined = jnp.dot(item_rows, w_item, preferred_element_type=jnp.float32).astype(jnp.bfloat16)
    item_terms = (
        jnp.dot(joined, w_joint, preferred_element_type=jnp.float32) + bias_hidden
    ).astype(jnp.bfloat16)
    return (queries, item_terms)


def score_pairs(queries, item_terms, key_rows, value_rows, is_valid, w_pooled, w_task, bias_task):
    scale = 1.0 / math.sqrt(queries.shape[-1])
    count_users, count_tokens, width = key_rows.shape
    flat_keys = key_rows.reshape(count_users * count_tokens, width)
    scores = jnp.einsum("id,nd->in", queries, flat_keys, preferred_element_type=jnp.float32) * scale
    scores = scores.reshape(queries.shape[0], count_users, count_tokens)
    scores = jnp.where(is_valid[None], scores, -jnp.inf)
    maximum = jnp.max(scores, axis=-1, keepdims=True)
    expo = jnp.exp(scores - maximum)
    weights = (expo / jnp.sum(expo, axis=-1, keepdims=True)).astype(jnp.bfloat16)
    pooled = jnp.einsum(
        "iut,utd->uid", weights, value_rows, preferred_element_type=jnp.float32
    ).astype(jnp.bfloat16)
    hidden = (
        jnp.einsum("uid,dh->uih", pooled, w_pooled, preferred_element_type=jnp.float32)
        + item_terms.astype(jnp.float32)[None]
    )
    hidden = jax.nn.relu(hidden).astype(jnp.bfloat16)
    logits = jnp.einsum("uih,hk->uki", hidden, w_task, preferred_element_type=jnp.float32)
    return logits + bias_task[None, :, None]


def shards(
    history,
    lengths,
    item_rows,
    w_query,
    w_item,
    w_key,
    w_value,
    w_pooled,
    w_joint,
    bias_hidden,
    w_task,
    bias_task,
):
    local = history.reshape(-1, DH)
    key_local = (
        jnp.dot(local, w_key, preferred_element_type=jnp.float32)
        .astype(jnp.bfloat16)
        .reshape(history.shape)
    )
    value_local = (
        jnp.dot(local, w_value, preferred_element_type=jnp.float32)
        .astype(jnp.bfloat16)
        .reshape(history.shape)
    )
    key_rows, value_rows = (
        lax.all_gather(key_local, "users", axis=1, tiled=True),
        lax.all_gather(value_local, "users", axis=1, tiled=True),
    )
    is_valid = jnp.arange(key_rows.shape[1], dtype=jnp.int32)[None, :] < lengths[:, None]

    def evaluate(arrived):
        queries, item_terms = project(arrived, w_query, w_item, w_joint, bias_hidden)
        return score_pairs(
            queries, item_terms, key_rows, value_rows, is_valid, w_pooled, w_task, bias_task
        )

    window = [None] * WIN
    window[REACH] = evaluate(item_rows)
    low_side = item_rows
    high_side = item_rows
    for offset in range(1, REACH + 1):
        low_side = shifted(low_side, "blk", 1)
        high_side = shifted(high_side, "blk", -1)
        window[REACH - offset] = evaluate(low_side)
        window[REACH + offset] = evaluate(high_side)
    return jnp.stack(window, axis=1)


def solution(mesh):
    placed = (
        P(("parts", "blk"), "users", None),
        P(("parts", "blk")),
        P(("parts", "blk", "users", "sub"), None),
        P(),
        P(),
        P(),
        P(),
        P(),
        P(),
        P(),
        P(),
        P(),
    )
    return jax.shard_map(
        shards,
        mesh=mesh,
        in_specs=placed,
        out_specs=P(("parts", "blk"), None, None, ("users", "sub")),
        check_vma=False,
    )
```

profile of v0, /device:TPU:0, one launch (start us, length us, event | category | flops | bytes accessed | tf_op | source)
XLA Modules:
  0.0 119.5 jit_solution(1426204656775976241)
XLA Ops:
  0.0 3.1 %collective-permute-start = (bf16[384,512]{1,0:T(8,128)(2,1)}, bf16[384,512]{1,0:T(8,128)(2,1)S(1)}, u32[]{:S(2)}, u32[]{:S(2)}) collective-permute-start(bf16[384,512]{1,0:T(8,128)(2,1)} %param.14), channel_id=1, source_target_pairs={{12,0},{0,4},{4,8},{8,12},{13,1},{1,5},{5,9},{9,13},{14,2},{2,6},{... | collective-permute-start | bytes 1179656 | tf_op jit(solution)/shard_map/ppermute | solution.py:16
  3.1 2.1 %collective-permute-start.4 = (bf16[384,512]{1,0:T(8,128)(2,1)}, bf16[384,512]{1,0:T(8,128)(2,1)S(1)}, u32[]{:S(2)}, u32[]{:S(2)}) collective-permute-start(bf16[384,512]{1,0:T(8,128)(2,1)} %param.14), channel_id=1, source_target_pairs={{4,0},{8,4},{12,8},{0,12},{5,1},{9,5},{13,9},{1,13},{6,2},{10,6},{... | collective-permute-start | bytes 1179656 | tf_op jit(solution)/shard_map/ppermute | solution.py:16
  5.2 1.1 convolution_convert_fusion.27
  6.3 5.6 %all_gather.7 = bf16[8,64,256]{2,1,0:T(8,128)(2,1)S(1)} all-gather(bf16[8,32,256]{2,1,0:T(8,128)(2,1)S(1)} %bitcast.219), channel_id=1, replica_groups=mesh['parts'=2,'blk'=4,'users'=2,'sub'=2] {'users'}, dimensions={1}, use_global_device_ids=true | all-gather | bytes 393216 | tf_op jit(solution)/shard_map/all_gather | solution.py:77
  12.0 1.2 convolution_convert_fusion.28
  13.1 5.6 %all_gather.6 = bf16[8,64,256]{2,1,0:T(8,128)(2,1)S(1)} all-gather(bf16[8,32,256]{2,1,0:T(8,128)(2,1)S(1)} %bitcast.220), channel_id=1, replica_groups=mesh['parts'=2,'blk'=4,'users'=2,'sub'=2] {'users'}, dimensions={1}, use_global_device_ids=true | all-gather | bytes 393216 | tf_op jit(solution)/shard_map/all_gather | solution.py:76
  18.9 0.6 convolution_multiply_fusion.4
  19.5 1.1 copy.18
  20.7 0.4 fusion.63
  21.1 0.7 copy-done.15
  22.1 2.3 %maximum_convert_fusion.4 = bf16[8,384,128]{2,1,0:T(8,128)(2,1)} fusion(bf16[8,64,256]{2,1,0:T(8,128)(2,1)S(1)} %all_gather.7, f32[384,128]{1,0:T(8,128)S(1)} %fusion.63, f32[384,8]{0,1:T(8,128)S(1)} %fusion.247, f32[384,8,64]{0,2,1:T(8,128)S(1)} %bitcast.216, pred[8,64]{1,0:T(8,128)(4,1)S(1)} %iota_compare_fusion, bf16[256,128]{1,0:T(8,128)(2,1)S(1)} %copy-done.19), kind=kOutput, calls=%fused_computation.22 | convolution fusion | flops 304745536 | bytes 2109952 | tf_op jit(solution)/shard_map/uid,dh->uih/dot_general | solution.py:42
  24.4 0.6 convolution_multiply_fusion.5
  24.9 1.1 copy.17
  26.1 1.4 %fusion.246 = f32[384,8]{0,1:T(8,128)S(1)} fusion(f32[384,8,64]{0,2,1:T(8,128)} %bitcast.213, pred[8,64]{1,0:T(8,128)(4,1)S(1)} %iota_compare_fusion), kind=kOutput, calls=%fused_computation.240 | output fusion | flops 589887 | bytes 799232 | tf_op jit(solution)/shard_map/sub | solution.py:36
  27.5 0.6 convolution_multiply_fusion.3
  28.1 1.2 copy.19
  29.7 3.4 %maximum_convert_fusion.5 = bf16[8,384,128]{2,1,0:T(8,128)(2,1)} fusion(bf16[8,64,256]{2,1,0:T(8,128)(2,1)S(1)} %all_gather.7, f32[384,128]{1,0:T(8,128)S(1)} %fusion.65, f32[384,8]{0,1:T(8,128)S(1)} %fusion.246, f32[384,8,64]{0,2,1:T(8,128)} %bitcast.214, pred[8,64]{1,0:T(8,128)(4,1)S(1)} %iota_compare_fusion, bf16[256,128]{1,0:T(8,128)(2,1)S(1)} %copy-done.19), kind=kOutput, calls=%fused_computation.23 | convolution fusion | flops 304745536 | bytes 2109952 | tf_op jit(solution)/shard_map/uid,dh->uih/dot_general | solution.py:42
  33.2 1.1 fusion.61
  34.3 3.8 %collective-permute-start.5 = (bf16[384,512]{1,0:T(8,128)(2,1)S(1)}, bf16[384,512]{1,0:T(8,128)(2,1)S(1)}, u32[]{:S(2)}, u32[]{:S(2)}) collective-permute-start(bf16[384,512]{1,0:T(8,128)(2,1)S(1)} %collective-permute-done.4), channel_id=1, source_target_pairs={{4,0},{8,4},{12,8},{0,12},{5,1},{9,5},{13,9},{1,13},{6,2},{10,6},{... | collective-permute-start | bytes 1179656 | tf_op jit(solution)/shard_map/ppermute | solution.py:16
  38.1 0.9 fusion.248
  39.0 3.2 %maximum_convert_fusion.3 = bf16[8,384,128]{2,1,0:T(8,128)(2,1)} fusion(bf16[8,64,256]{2,1,0:T(8,128)(2,1)S(1)} %all_gather.7, f32[384,128]{1,0:T(8,128)} %fusion.61, f32[384,8]{0,1:T(8,128)} %fusion.248, f32[384,8,64]{0,2,1:T(8,128)S(1)} %bitcast.202, pred[8,64]{1,0:T(8,128)(4,1)S(1)} %iota_compare_fusion, bf16[256,128]{1,0:T(8,128)(2,1)S(1)} %copy-done.19), kind=kOutput, calls=%fused_computation.21 | convolution fusion | flops 304745536 | bytes 2109952 | tf_op jit(solution)/shard_map/uid,dh->uih/dot_general | solution.py:42
  42.2 4.8 %collective-permute-done.1 = bf16[384,512]{1,0:T(8,128)(2,1)S(1)} collective-permute-done((bf16[384,512]{1,0:T(8,128)(2,1)S(1)}, bf16[384,512]{1,0:T(8,128)(2,1)S(1)}, u32[]{:S(2)}, u32[]{:S(2)}) %collective-permute-start.1) | collective-permute-done | bytes 393248 | tf_op jit(solution)/shard_map/ppermute | solution.py:16
  47.0 0.6 convolution_multiply_fusion.6
  47.6 1.1 copy.16
  48.7 1.4 %fusion.245 = f32[384,8]{0,1:T(8,128)S(1)} fusion(f32[384,8,64]{0,2,1:T(8,128)} %bitcast.209, pred[8,64]{1,0:T(8,128)(4,1)S(1)} %iota_compare_fusion), kind=kOutput, calls=%fused_computation.239 | output fusion | flops 589887 | bytes 799232 | tf_op jit(solution)/shard_map/sub | solution.py:36
  50.2 1.4 %collective-permute-done.5 = bf16[384,512]{1,0:T(8,128)(2,1)S(1)} collective-permute-done((bf16[384,512]{1,0:T(8,128)(2,1)S(1)}, bf16[384,512]{1,0:T(8,128)(2,1)S(1)}, u32[]{:S(2)}, u32[]{:S(2)}) %collective-permute-start.5) | collective-permute-done | bytes 393248 | tf_op jit(solution)/shard_map/ppermute | solution.py:16
  51.5 0.6 convolution_multiply_fusion.2
  52.1 1.2 copy.20
  53.3 0.4 fusion.67
  53.7 3.4 %maximum_convert_fusion.6 = bf16[8,384,128]{2,1,0:T(8,128)(2,1)} fusion(bf16[8,64,256]{2,1,0:T(8,128)(2,1)S(1)} %all_gather.7, f32[384,128]{1,0:T(8,128)S(1)} %fusion.67, f32[384,8]{0,1:T(8,128)S(1)} %fusion.245, f32[384,8,64]{0,2,1:T(8,128)} %bitcast.210, pred[8,64]{1,0:T(8,128)(4,1)S(1)} %iota_compare_fusion, bf16[256,128]{1,0:T(8,128)(2,1)S(1)} %copy-done.19), kind=kOutput, calls=%fused_computation.24 | convolution fusion | flops 304745536 | bytes 2109952 | tf_op jit(solution)/shard_map/uid,dh->uih/dot_general | solution.py:42
  57.1 1.0 collective-permute-start.2
  58.1 1.1 fusion.59
  59.2 2.9 %collective-permute-start.6 = (bf16[384,512]{1,0:T(8,128)(2,1)S(1)}, bf16[384,512]{1,0:T(8,128)(2,1)S(1)}, u32[]{:S(2)}, u32[]{:S(2)}) collective-permute-start(bf16[384,512]{1,0:T(8,128)(2,1)S(1)} %collective-permute-done.5), channel_id=1, source_target_pairs={{4,0},{8,4},{12,8},{0,12},{5,1},{9,5},{13,9},{1,13},{6,2},{10,6},{... | collective-permute-start | bytes 1179656 | tf_op jit(solution)/shard_map/ppermute | solution.py:16
  62.1 0.9 fusion.249
  63.0 3.3 %maximum_convert_fusion.2 = bf16[8,384,128]{2,1,0:T(8,128)(2,1)} fusion(bf16[8,64,256]{2,1,0:T(8,128)(2,1)S(1)} %all_gather.7, f32[384,128]{1,0:T(8,128)} %fusion.59, f32[384,8]{0,1:T(8,128)} %fusion.249, f32[384,8,64]{0,2,1:T(8,128)S(1)} %bitcast.204, pred[8,64]{1,0:T(8,128)(4,1)S(1)} %iota_compare_fusion, bf16[256,128]{1,0:T(8,128)(2,1)S(1)} %copy-done.19), kind=kOutput, calls=%fused_computation.20 | convolution fusion | flops 304745536 | bytes 2109952 | tf_op jit(solution)/shard_map/uid,dh->uih/dot_general | solution.py:42
  66.2 4.8 %collective-permute-done.2 = bf16[384,512]{1,0:T(8,128)(2,1)S(1)} collective-permute-done((bf16[384,512]{1,0:T(8,128)(2,1)S(1)}, bf16[384,512]{1,0:T(8,128)(2,1)S(1)}, u32[]{:S(2)}, u32[]{:S(2)}) %collective-permute-start.2) | collective-permute-done | bytes 393248 | tf_op jit(solution)/shard_map/ppermute | solution.py:16
  71.0 0.6 convolution_multiply_fusion.7
  71.6 1.1 copy.15
  72.8 1.4 %fusion.244 = f32[384,8]{0,1:T(8,128)S(1)} fusion(f32[384,8,64]{0,2,1:T(8,128)} %bitcast.211, pred[8,64]{1,0:T(8,128)(4,1)S(1)} %iota_compare_fusion), kind=kOutput, calls=%fused_computation.238 | output fusion | flops 589887 | bytes 799232 | tf_op jit(solution)/shard_map/sub | solution.py:36
  74.2 3.4 %collective-permute-done.6 = bf16[384,512]{1,0:T(8,128)(2,1)S(1)} collective-permute-done((bf16[384,512]{1,0:T(8,128)(2,1)S(1)}, bf16[384,512]{1,0:T(8,128)(2,1)S(1)}, u32[]{:S(2)}, u32[]{:S(2)}) %collective-permute-start.6) | collective-permute-done | bytes 393248 | tf_op jit(solution)/shard_map/ppermute | solution.py:16
  77.6 0.6 convolution_multiply_fusion.1
  78.2 1.1 copy.21
  79.8 3.5 %maximum_convert_fusion.7 = bf16[8,384,128]{2,1,0:T(8,128)(2,1)} fusion(bf16[8,64,256]{2,1,0:T(8,128)(2,1)S(1)} %all_gather.7, f32[384,128]{1,0:T(8,128)S(1)} %fusion.69, f32[384,8]{0,1:T(8,128)S(1)} %fusion.244, f32[384,8,64]{0,2,1:T(8,128)} %bitcast.212, pred[8,64]{1,0:T(8,128)(4,1)S(1)} %iota_compare_fusion, bf16[256,128]{1,0:T(8,128)(2,1)S(1)} %copy-done.19), kind=kOutput, calls=%fused_computation.25 | convolution fusion | flops 304745536 | bytes 2109952 | tf_op jit(solution)/shard_map/uid,dh->uih/dot_general | solution.py:42
  83.3 0.5 collective-permute-start.3
  83.8 1.1 fusion.57
  84.9 3.3 %collective-permute-start.7 = (bf16[384,512]{1,0:T(8,128)(2,1)S(1)}, bf16[384,512]{1,0:T(8,128)(2,1)S(1)}, u32[]{:S(2)}, u32[]{:S(2)}) collective-permute-start(bf16[384,512]{1,0:T(8,128)(2,1)S(1)} %collective-permute-done.6), channel_id=1, source_target_pairs={{4,0},{8,4},{12,8},{0,12},{5,1},{9,5},{13,9},{1,13},{6,2},{10,6},{... | collective-permute-start | bytes 1179656 | tf_op jit(solution)/shard_map/ppermute | solution.py:16
  88.2 0.9 fusion.250
  89.1 3.2 %maximum_convert_fusion.1 = bf16[8,384,128]{2,1,0:T(8,128)(2,1)} fusion(bf16[8,64,256]{2,1,0:T(8,128)(2,1)S(1)} %all_gather.7, f32[384,128]{1,0:T(8,128)} %fusion.57, f32[384,8]{0,1:T(8,128)} %fusion.250, f32[384,8,64]{0,2,1:T(8,128)S(1)} %bitcast.206, pred[8,64]{1,0:T(8,128)(4,1)S(1)} %iota_compare_fusion, bf16[256,128]{1,0:T(8,128)(2,1)S(1)} %copy-done.19), kind=kOutput, calls=%fused_computation.19 | convolution fusion | flops 304745536 | bytes 2109952 | tf_op jit(solution)/shard_map/uid,dh->uih/dot_general | solution.py:42
  92.3 4.8 %collective-permute-done.3 = bf16[384,512]{1,0:T(8,128)(2,1)S(1)} collective-permute-done((bf16[384,512]{1,0:T(8,128)(2,1)S(1)}, bf16[384,512]{1,0:T(8,128)(2,1)S(1)}, u32[]{:S(2)}, u32[]{:S(2)}) %collective-permute-start.3) | collective-permute-done | bytes 393248 | tf_op jit(solution)/shard_map/ppermute | solution.py:16
  97.1 0.6 convolution_multiply_fusion.8
  97.7 1.1 copy.14
  98.8 2.0 %fusion.243 = f32[384,8]{0,1:T(8,128)} fusion(f32[384,8,64]{0,2,1:T(8,128)} %bitcast.207, pred[8,64]{1,0:T(8,128)(4,1)S(1)} %iota_compare_fusion), kind=kOutput, calls=%fused_computation.237 | output fusion | flops 589887 | bytes 799232 | tf_op jit(solution)/shard_map/sub | solution.py:36
  100.8 3.3 %collective-permute-done.7 = bf16[384,512]{1,0:T(8,128)(2,1)S(1)} collective-permute-done((bf16[384,512]{1,0:T(8,128)(2,1)S(1)}, bf16[384,512]{1,0:T(8,128)(2,1)S(1)}, u32[]{:S(2)}, u32[]{:S(2)}) %collective-permute-start.7) | collective-permute-done | bytes 393248 | tf_op jit(solution)/shard_map/ppermute | solution.py:16
  104.1 0.6 convolution_multiply_fusion
  105.0 0.9 fusion.251
  105.9 0.4 fusion.71
  106.3 3.5 %maximum_convert_fusion.8 = bf16[8,384,128]{2,1,0:T(8,128)(2,1)} fusion(bf16[8,64,256]{2,1,0:T(8,128)(2,1)S(1)} %all_gather.7, f32[384,128]{1,0:T(8,128)S(1)} %fusion.71, f32[384,8]{0,1:T(8,128)S(1)} %copy-done.22, f32[384,8,64]{0,2,1:T(8,128)} %bitcast.208, pred[8,64]{1,0:T(8,128)(4,1)S(1)} %iota_compare_fusion, bf16[256,128]{1,0:T(8,128)(2,1)S(1)} %copy-done.19), kind=kOutput, calls=%fused_computation.26 | convolution fusion | flops 304745536 | bytes 2109952 | tf_op jit(solution)/shard_map/uid,dh->uih/dot_general | solution.py:42
  109.9 1.5 %fusion.89 = f32[8,9,8,384]{3,2,0,1:T(8,128)S(1)} fusion(bf16[8,384,128]{2,1,0:T(8,128)(2,1)} %maximum_convert_fusion.8, f32[8]{0:T(128)S(1)} %copy-done.18, bf16[128,8]{0,1:T(8,128)(2,1)S(1)} %copy-done.16), kind=kOutput, calls=%fused_computation.145 | convolution fusion | flops 6316031 | bytes 886816 | tf_op jit(solution)/shard_map/uih,hk->uki/dot_general | solution.py:46
  112.0 0.5 copy-done.5
  113.2 0.5 copy-done.6
  114.4 0.5 copy-done.9
  115.2 0.4 fusion.55
  115.7 2.5 %maximum_convert_fusion = bf16[8,384,128]{2,1,0:T(8,128)(2,1)S(1)} fusion(bf16[8,64,256]{2,1,0:T(8,128)(2,1)S(1)} %all_gather.7, f32[384,128]{1,0:T(8,128)S(1)} %fusion.55, f32[384,8]{0,1:T(8,128)S(1)} %copy-done.21, f32[384,8,64]{0,2,1:T(8,128)} %bitcast.200, pred[8,64]{1,0:T(8,128)(4,1)S(1)} %iota_compare_fusion, bf16[256,128]{1,0:T(8,128)(2,1)S(1)} %copy-done.19), kind=kOutput, calls=%fused_computation.18 | convolution fusion | flops 304745536 | bytes 2109952 | tf_op jit(solution)/shard_map/uid,dh->uih/dot_general | solution.py:42
  118.5 1.0 copy.23
  (58 shorter events, 4.2 us)
Async XLA Ops:
  0.0 18.9 %copy-start = (bf16[512,256]{1,0:T(8,128)(2,1)S(1)}, bf16[512,256]{1,0:T(8,128)(2,1)}, u32[]{:S(2)}) copy-start(bf16[512,256]{1,0:T(8,128)(2,1)} %param.15) | copy-start | bytes 786436
  0.0 18.9 %copy-start.3 = (bf16[384,512]{1,0:T(8,128)(2,1)S(1)}, bf16[384,512]{1,0:T(8,128)(2,1)}, u32[]{:S(2)}) copy-start(bf16[384,512]{1,0:T(8,128)(2,1)} %param.14) | copy-start | bytes 1179652
  0.0 18.8 %copy-start.20 = (s32[8]{0:T(128)S(1)}, s32[8]{0:T(128)}, u32[]{:S(2)}) copy-start(s32[8]{0:T(128)} %param.13) | copy-start | bytes 100
  0.0 24.4 %collective-permute-start = (bf16[384,512]{1,0:T(8,128)(2,1)}, bf16[384,512]{1,0:T(8,128)(2,1)S(1)}, u32[]{:S(2)}, u32[]{:S(2)}) collective-permute-start(bf16[384,512]{1,0:T(8,128)(2,1)} %param.14), channel_id=1, source_target_pairs={{12,0},{0,4},{4,8},{8,12},{13,1},{1,5},{5,9},{9,13},{14,2},{2,6},{... | collective-permute-start | bytes 1179656 | tf_op jit(solution)/shard_map/ppermute | solution.py:16
  3.1 24.4 %collective-permute-start.4 = (bf16[384,512]{1,0:T(8,128)(2,1)}, bf16[384,512]{1,0:T(8,128)(2,1)S(1)}, u32[]{:S(2)}, u32[]{:S(2)}) collective-permute-start(bf16[384,512]{1,0:T(8,128)(2,1)} %param.14), channel_id=1, source_target_pairs={{4,0},{8,4},{12,8},{0,12},{5,1},{9,5},{13,9},{1,13},{6,2},{10,6},{... | collective-permute-start | bytes 1179656 | tf_op jit(solution)/shard_map/ppermute | solution.py:16
  19.4 1.2 copy-start.1
  19.5 1.2 copy-start.2
  19.5 1.2 copy-start.17
  20.6 1.1 copy-start.15
  20.6 1.4 %copy-start.19 = (bf16[256,128]{1,0:T(8,128)(2,1)S(1)}, bf16[256,128]{1,0:T(8,128)(2,1)}, u32[]{:S(2)}) copy-start(bf16[256,128]{1,0:T(8,128)(2,1)} %param.19) | copy-start | bytes 196612
  33.1 4.9 %copy-start.12 = (f32[384,512]{0,1:T(8,128)S(1)}, f32[384,512]{0,1:T(8,128)}, u32[]{:S(2)}) copy-start(f32[384,512]{0,1:T(8,128)} %copy.19) | copy-start | bytes 2359300
  33.1 13.9 %collective-permute-start.1 = (bf16[384,512]{1,0:T(8,128)(2,1)S(1)}, bf16[384,512]{1,0:T(8,128)(2,1)S(1)}, u32[]{:S(2)}, u32[]{:S(2)}) collective-permute-start(bf16[384,512]{1,0:T(8,128)(2,1)S(1)} %collective-permute-done), channel_id=1, source_target_pairs={{12,0},{0,4},{4,8},{8,12},{13,1},{1,5},{5,9},{9,13},{14,2},{2,6},{... | collective-permute-start | bytes 1179656 | tf_op jit(solution)/shard_map/ppermute | solution.py:16
  34.3 17.3 %collective-permute-start.5 = (bf16[384,512]{1,0:T(8,128)(2,1)S(1)}, bf16[384,512]{1,0:T(8,128)(2,1)S(1)}, u32[]{:S(2)}, u32[]{:S(2)}) collective-permute-start(bf16[384,512]{1,0:T(8,128)(2,1)S(1)} %collective-permute-done.4), channel_id=1, source_target_pairs={{4,0},{8,4},{12,8},{0,12},{5,1},{9,5},{13,9},{1,13},{6,2},{10,6},{... | collective-permute-start | bytes 1179656 | tf_op jit(solution)/shard_map/ppermute | solution.py:16
  57.1 4.9 %copy-start.13 = (f32[384,512]{0,1:T(8,128)S(1)}, f32[384,512]{0,1:T(8,128)}, u32[]{:S(2)}) copy-start(f32[384,512]{0,1:T(8,128)} %copy.20) | copy-start | bytes 2359300
  57.1 13.9 %collective-permute-start.2 = (bf16[384,512]{1,0:T(8,128)(2,1)S(1)}, bf16[384,512]{1,0:T(8,128)(2,1)S(1)}, u32[]{:S(2)}, u32[]{:S(2)}) collective-permute-start(bf16[384,512]{1,0:T(8,128)(2,1)S(1)} %collective-permute-done.1), channel_id=1, source_target_pairs={{12,0},{0,4},{4,8},{8,12},{13,1},{1,5},{5,9},{9,13},{14,2},{2,6},{... | collective-permute-start | bytes 1179656 | tf_op jit(solution)/shard_map/ppermute | solution.py:16
  59.2 18.4 %collective-permute-start.6 = (bf16[384,512]{1,0:T(8,128)(2,1)S(1)}, bf16[384,512]{1,0:T(8,128)(2,1)S(1)}, u32[]{:S(2)}, u32[]{:S(2)}) collective-permute-start(bf16[384,512]{1,0:T(8,128)(2,1)S(1)} %collective-permute-done.5), channel_id=1, source_target_pairs={{4,0},{8,4},{12,8},{0,12},{5,1},{9,5},{13,9},{1,13},{6,2},{10,6},{... | collective-permute-start | bytes 1179656 | tf_op jit(solution)/shard_map/ppermute | solution.py:16
  83.3 4.9 %copy-start.14 = (f32[384,512]{0,1:T(8,128)S(1)}, f32[384,512]{0,1:T(8,128)}, u32[]{:S(2)}) copy-start(f32[384,512]{0,1:T(8,128)} %copy.21) | copy-start | bytes 2359300
  83.3 13.8 %collective-permute-start.3 = (bf16[384,512]{1,0:T(8,128)(2,1)S(1)}, bf16[384,512]{1,0:T(8,128)(2,1)S(1)}, u32[]{:S(2)}, u32[]{:S(2)}) collective-permute-start(bf16[384,512]{1,0:T(8,128)(2,1)S(1)} %collective-permute-done.2), channel_id=1, source_target_pairs={{12,0},{0,4},{4,8},{8,12},{13,1},{1,5},{5,9},{9,13},{14,2},{2,6},{... | collective-permute-start | bytes 1179656 | tf_op jit(solution)/shard_map/ppermute | solution.py:16
  84.9 19.2 %collective-permute-start.7 = (bf16[384,512]{1,0:T(8,128)(2,1)S(1)}, bf16[384,512]{1,0:T(8,128)(2,1)S(1)}, u32[]{:S(2)}, u32[]{:S(2)}) collective-permute-start(bf16[384,512]{1,0:T(8,128)(2,1)S(1)} %collective-permute-done.6), channel_id=1, source_target_pairs={{4,0},{8,4},{12,8},{0,12},{5,1},{9,5},{13,9},{1,13},{6,2},{10,6},{... | collective-permute-start | bytes 1179656 | tf_op jit(solution)/shard_map/ppermute | solution.py:16
  105.0 1.3 %copy-start.11 = (f32[384,512]{0,1:T(8,128)}, f32[384,512]{0,1:T(8,128)S(1)}, u32[]{:S(2)}) copy-start(f32[384,512]{0,1:T(8,128)S(1)} %copy.22) | copy-start | bytes 2359300
  105.0 1.3 %copy-start.22 = (f32[384,8]{0,1:T(8,128)S(1)}, f32[384,8]{0,1:T(8,128)}, u32[]{:S(2)}) copy-start(f32[384,8]{0,1:T(8,128)} %fusion.243) | copy-start | bytes 36868
  106.3 3.5 %copy-start.16 = (bf16[128,8]{0,1:T(8,128)(2,1)S(1)}, bf16[128,8]{0,1:T(8,128)(2,1)}, u32[]{:S(2)}) copy-start(bf16[128,8]{0,1:T(8,128)(2,1)} %param.22) | copy-start | bytes 6148
  106.3 3.5 %copy-start.18 = (f32[8]{0:T(128)S(1)}, f32[8]{0:T(128)}, u32[]{:S(2)}) copy-start(f32[8]{0:T(128)} %param.23) | copy-start | bytes 100
  106.3 5.0 %copy-start.10 = (bf16[8,384,128]{2,1,0:T(8,128)(2,1)S(1)}, bf16[8,384,128]{2,1,0:T(8,128)(2,1)}, u32[]{:S(2)}) copy-start(bf16[8,384,128]{2,1,0:T(8,128)(2,1)} %maximum_convert_fusion.7) | copy-start | bytes 2359300
  109.9 1.8 %copy-start.7 = (bf16[8,384,128]{2,1,0:T(8,128)(2,1)S(1)}, bf16[8,384,128]{2,1,0:T(8,128)(2,1)}, u32[]{:S(2)}) copy-start(bf16[8,384,128]{2,1,0:T(8,128)(2,1)} %maximum_convert_fusion.6) | copy-start | bytes 2359300
  111.4 1.2 copy-start.5
  111.7 1.2 %copy-start.4 = (bf16[8,384,128]{2,1,0:T(8,128)(2,1)S(1)}, bf16[8,384,128]{2,1,0:T(8,128)(2,1)}, u32[]{:S(2)}) copy-start(bf16[8,384,128]{2,1,0:T(8,128)(2,1)} %maximum_convert_fusion.4) | copy-start | bytes 2359300
  112.5 1.2 copy-start.6
  112.9 1.2 copy-start.8
  113.7 1.2 copy-start.9
  114.9 0.8 copy-start.21
where the time goes:
time: 120 us
  matrix products  45.7 us (38%)
  waiting for transfers between devices  22.5 us (19%)
  starting transfers between devices  16.6 us (14%)
  local copies, waits for them, and re-layouts  12.9 us (11%)
  blocking collectives  11.3 us (9%)
  other arithmetic  10.2 us (8%)
    dot_general x9, matrix products, score_pairs(): jnp.einsum('uid,dh->uih', pooled, w_pooled, preferred_element_type=jnp.fl...  28.4 us
    ppermute x8, waiting for transfers between devices, shifted(): return lax.ppermute(block, axis, route)  22.5 us
    ppermute x8, starting transfers between devices, shifted(): return lax.ppermute(block, axis, route)  16.6 us
    sub x9, other arithmetic, score_pairs(): expo = jnp.exp(scores - maximum)  10.1 us
    mul x9, local copies, waits for them, and re-layouts, score_pairs(): jnp.einsum('id,nd->in', queries, flat_keys, preferred_element_type=jnp.fl...  9.49 us
    dot_general x9, matrix products, project(): jnp.dot(joined, w_joint, preferred_element_type=jnp.float32) + bias_hidden  5.92 us
    all_gather x1, blocking collectives, shards(): lax.all_gather(key_local, 'users', axis=1, tiled=True)  5.64 us
    all_gather x1, blocking collectives, shards(): lax.all_gather(value_local, 'users', axis=1, tiled=True)  5.64 us
  transfers between devices with their start and end apart: 8, of which 6 were waited for; matrix products, arithmetic and copies ran while one was open for 30% of the time, Pallas kernels for 0%

commit v1 on v0

v1 whole, which is shorter than its diff:
```python
import functools
import math

import jax
import jax.numpy as jnp
from jax import lax
from jax.experimental import pallas as pl
from jax.experimental.pallas import tpu as pltpu
from jax.sharding import PartitionSpec as P

REACH = 4
WIN = 2 * REACH + 1
LEN_ROWS = 16
F32, BF16 = jnp.float32, jnp.bfloat16


def offsets_of(n_blk):
    if n_blk >= WIN:
        return [k - REACH for k in range(WIN)], list(range(WIN))
    return list(range(n_blk)), [(k - REACH) % n_blk for k in range(WIN)]


def mm(a, b, dims=((1,), (0,))):
    return lax.dot_general(a, b, (dims, ((), ())), preferred_element_type=F32)


def kernel(
    n_blk, n_x, n_sub, hist, lens, items, w_query, w_item, w_key, w_value, w_pooled, w_joint,
    bias_hidden, w_task, bias_task, out, tokens, projected, terms, results,
    z_send, z_recv, x_send, x_recv, c_send, c_recv, r_send, r_recv,
):
    offsets, _ = offsets_of(n_blk)
    own = offsets.index(0)
    order = sorted(range(len(offsets)), key=lambda s: min(offsets[s] % n_blk, -offsets[s] % n_blk))
    users, held, width = hist.shape
    count = users // n_sub
    rows = count * held
    n_items = items.shape[0]
    all_items = n_sub * n_items
    n_hid, n_task = w_task.shape
    me, x, c = lax.axis_index("blk"), lax.axis_index("users"), lax.axis_index("sub")

    def blk_at(distance):
        return lax.rem(me + distance % n_blk, n_blk)

    def x_at(distance):
        return lax.rem(x + distance % n_x, n_x)

    def sub_at(distance):
        return lax.rem(c + distance % n_sub, n_sub)

    tokens[own, x, :rows, :] = hist[pl.ds(c * count, count)].reshape(rows, width)
    row = lax.broadcasted_iota(jnp.int32, (LEN_ROWS, width), 0)
    length_rows = jnp.zeros((LEN_ROWS, width), F32)
    for u in range(count):
        length_rows = jnp.where(row == u, lens[c * count + u].astype(F32), length_rows)
    tokens[own, x, rows:, :] = length_rows.astype(BF16)

    barrier = pltpu.get_barrier_semaphore()
    greeted = 0
    for o in offsets:
        for j in range(n_sub):
            if o != 0 or j != 0:
                target = {"blk": blk_at(o), "sub": sub_at(j)}
                pl.semaphore_signal(barrier, inc=1, device_id=target)
                greeted += 1
    for j in range(1, n_x):
        pl.semaphore_signal(barrier, inc=1, device_id={"users": x_at(j)})
        greeted += 1
    pl.semaphore_wait(barrier, greeted)

    def along_blk(s):
        return pltpu.make_async_remote_copy(
            tokens.at[own, x], tokens.at[s, x], z_send.at[s], z_recv.at[s],
            device_id={"blk": blk_at(offsets[s])},
        )

    def along_x(s, j):
        return pltpu.make_async_remote_copy(
            tokens.at[s, x], tokens.at[s, x], x_send.at[s, j], x_recv.at[s, j],
            device_id={"users": x_at(j)},
        )

    def from_x(s, j):
        there = tokens.at[s, x_at(-j)]
        return pltpu.make_async_remote_copy(
            there, there, x_send.at[s, j], x_recv.at[s, j], device_id={"users": x_at(j)}
        )

    def along_sub(j):
        return pltpu.make_async_remote_copy(
            projected.at[c], projected.at[c], c_send.at[j], c_recv.at[j],
            device_id={"sub": sub_at(j)},
        )

    def from_sub(j):
        there = projected.at[sub_at(-j)]
        return pltpu.make_async_remote_copy(
            there, there, c_send.at[j], c_recv.at[j], device_id={"sub": sub_at(j)}
        )

    def back(s, j):
        source, target = results.at[s, sub_at(j)], out.at[s, c]
        if s == own and j == 0:
            return pltpu.make_async_copy(source, target, r_send.at[s, j])
        return pltpu.make_async_remote_copy(
            source, target, r_send.at[s, j], r_recv.at[s, j],
            device_id={"blk": blk_at(-offsets[s]), "sub": sub_at(j)},
        )

    def from_back(s, j):
        return pltpu.make_async_remote_copy(
            results.at[s, sub_at(j)], out.at[s, sub_at(-j)], r_send.at[s, j], r_recv.at[s, j],
            device_id={"blk": blk_at(-offsets[s]), "sub": sub_at(j)},
        )

    for j in range(1, n_x):
        along_x(own, j).start()
    for s in order[1:]:
        along_blk(s).start()

    item_rows = items[...]
    projected[c, :, :width] = mm(item_rows, w_query[...]).astype(BF16)
    joined = mm(item_rows, w_item[...]).astype(BF16)
    projected[c, :, width:] = (mm(joined, w_joint[...]) + bias_hidden[...][None, :]).astype(BF16)
    for j in range(1, n_sub):
        along_sub(j).start()
    for j in range(1, n_sub):
        from_sub(j).wait_recv()
    for j in range(n_sub):
        terms[:, j * n_items : (j + 1) * n_items] = projected[j, :, width:].astype(F32).T

    head = w_task[...].astype(F32).T
    nothing = jnp.zeros_like(head)
    heads = jnp.concatenate(
        [jnp.concatenate([head, nothing], 1), jnp.concatenate([nothing, head], 1)], 0
    ).astype(BF16)
    row = lax.broadcasted_iota(jnp.int32, (2 * n_task, n_items), 0)
    bias = jnp.zeros((2 * n_task, n_items), F32)
    for t in range(n_task):
        bias = jnp.where((row == t) | (row == t + n_task), bias_task[t], bias)

    factor = math.log2(math.e) / math.sqrt(width)
    place = lax.broadcasted_iota(jnp.int32, (n_x * held, all_items), 0).astype(F32)

    def score(s):
        block = tokens[s, :, :rows, :].reshape(n_x * rows, width)
        keys = mm(block, w_key[...]).astype(BF16)
        values = mm(block, w_value[...]).astype(BF16)
        pooled_values = mm(values, w_pooled[...]).astype(BF16)
        valid_count = tokens[s, 0, rows:, :128].astype(F32)
        queries = projected[:, :, :width].reshape(all_items, width)

        def of_user(array, u):
            return jnp.concatenate(
                [array[p * rows + u * held : p * rows + (u + 1) * held] for p in range(n_x)], 0
            )

        for first in range(0, count, 2):
            hidden = []
            for u in (first, first + 1):
                scores = mm(of_user(keys, u), queries, ((1,), (1,)))
                limit = jnp.concatenate([valid_count[u : u + 1]] * (all_items // 128), 1)
                scores = jnp.where(place < limit, scores, -jnp.inf)
                expo = jnp.exp2((scores - jnp.max(scores, 0, keepdims=True)) * factor)
                weights = (expo * (1.0 / jnp.sum(expo, 0, keepdims=True))).astype(BF16)
                layer = mm(of_user(pooled_values, u), weights, ((0,), (0,))) + terms[...]
                hidden.append(jnp.maximum(layer, 0.0).astype(BF16))
            logits = mm(heads, jnp.concatenate(hidden, 0))
            for j in range(n_sub):
                results[s, j, first * n_task : (first + 2) * n_task, :] = (
                    logits[:, j * n_items : (j + 1) * n_items] + bias
                ).astype(BF16)

    for place_in_order, s in enumerate(order):
        if place_in_order + 1 < len(order):
            later = order[place_in_order + 1]
            along_blk(later).wait_recv()
            for j in range(1, n_x):
                along_x(later, j).start()
        for j in range(1, n_x):
            from_x(s, j).wait_recv()
        score(s)
        for j in range(n_sub):
            back(s, j).start()

    for s in order:
        if s != own:
            along_blk(s).wait_send()
        for j in range(1, n_x):
            along_x(s, j).wait_send()
        for j in range(n_sub):
            if s == own and j == 0:
                back(s, j).wait()
            else:
                back(s, j).wait_send()
                from_back(s, j).wait_recv()
    for j in range(1, n_sub):
        along_sub(j).wait_send()


def shards(
    n_blk, n_x, n_sub, history, lengths, item_rows, w_query, w_item, w_key, w_value, w_pooled,
    w_joint, bias_hidden, w_task, bias_task,
):
    offsets, place_of = offsets_of(n_blk)
    users, held, width = history.shape
    n_items = item_rows.shape[0]
    n_hid, n_task = w_task.shape
    n_slots, count = len(offsets), users // n_sub
    vmem, smem = pl.BlockSpec(memory_space=pltpu.VMEM), pl.BlockSpec(memory_space=pltpu.SMEM)
    dma = pltpu.SemaphoreType.DMA
    by_offset = pl.pallas_call(
        functools.partial(kernel, n_blk, n_x, n_sub),
        out_shape=jax.ShapeDtypeStruct((n_slots, n_sub, count * n_task, n_items), BF16),
        in_specs=[vmem, smem] + [vmem] * 9 + [smem],
        out_specs=pl.BlockSpec(memory_space=pl.ANY),
        scratch_shapes=[
            pltpu.VMEM((n_slots, n_x, count * held + LEN_ROWS, width), BF16),
            pltpu.VMEM((n_sub, n_items, width + n_hid), BF16),
            pltpu.VMEM((n_hid, n_sub * n_items), F32),
            pltpu.VMEM((n_slots, n_sub, count * n_task, n_items), BF16),
            dma((n_slots,)),
            dma((n_slots,)),
            dma((n_slots, n_x)),
            dma((n_slots, n_x)),
            dma((n_sub,)),
            dma((n_sub,)),
            dma((n_slots, n_sub)),
            dma((n_slots, n_sub)),
        ],
        compiler_params=pltpu.CompilerParams(
            collective_id=0, has_side_effects=True, vmem_limit_bytes=40 * 1024 * 1024
        ),
        name="score_users",
    )(
        history, lengths, item_rows, w_query, w_item, w_key, w_value, w_pooled, w_joint,
        bias_hidden, w_task, bias_task,
    )
    by_offset = by_offset.reshape(n_slots, users, n_task, n_items).astype(F32)
    return jnp.stack([by_offset[s] for s in place_of], axis=1)


def solution(mesh):
    placed = (
        P(("parts", "blk"), "users", None),
        P(("parts", "blk")),
        P(("parts", "blk", "users", "sub"), None),
    ) + (P(),) * 9
    sizes = (mesh.shape["blk"], mesh.shape["users"], mesh.shape["sub"])
    return jax.shard_map(
        functools.partial(shards, *sizes),
        mesh=mesh,
        in_specs=placed,
        out_specs=P(("parts", "blk"), None, None, ("users", "sub")),
        check_vma=False,
    )
```

time: 120 us -> 34.1 us (0.28)
  matrix products: 45.7 us -> 0 us
  Pallas kernels: 0 us -> 23.7 us
  waiting for transfers between devices: 22.5 us -> 0 us
  starting transfers between devices: 16.6 us -> 0 us
  blocking collectives: 11.3 us -> 0 us
  other arithmetic: 10.2 us -> 0 us
  local copies, waits for them, and re-layouts: 12.9 us -> 9.79 us
    dot_general x38 -> x0, matrix products: 45.7 us -> none  [the longest x9 28.4 us: score_pairs(): jnp.einsum('uid,dh->uih', pooled, w_pooled, preferred_element_type=jnp.fl...]
    pallas_call x0 -> x1, Pallas kernels: none -> 23.7 us  [shards(): pl.pallas_call(functools.partial(kernel, n_blk, n_x, n_sub), out_shape=ja...]
    ppermute x8 -> x0, waiting for transfers between devices: 22.5 us -> none  [shifted(): return lax.ppermute(block, axis, route)]
    ppermute x8 -> x0, starting transfers between devices: 16.6 us -> none  [shifted(): return lax.ppermute(block, axis, route)]
    all_gather x2 -> x0, blocking collectives: 11.3 us -> none  [the longest x1 5.64 us: shards(): lax.all_gather(key_local, 'users', axis=1, tiled=True)]
    sub x9 -> x0, other arithmetic: 10.1 us -> none  [score_pairs(): expo = jnp.exp(scores - maximum)]
    mul x9 -> x0, local copies, waits for them, and re-layouts: 9.49 us -> none  [score_pairs(): jnp.einsum('id,nd->in', queries, flat_keys, preferred_element_type=jnp.fl...]
    unnamed x46 -> x33, local copies, waits for them, and re-layouts: 2.44 us -> 9.11 us
  transfers between devices with their start and end apart: 8 -> 0, of which waited for: 6 -> 0; matrix products, arithmetic and copies ran while one was open for 30% -> 0% of each run, Pallas kernels for 0% -> 0%
where the time goes in v1:
time: 34.1 us; the launch traced here: 33.6 us
  Pallas kernels  23.7 us (70%)
  local copies, waits for them, and re-layouts  9.79 us (29%)
    pallas_call x1, Pallas kernels, shards(): pl.pallas_call(functools.partial(kernel, n_blk, n_x, n_sub), out_shape=ja...  23.7 us
    unnamed x33, local copies, waits for them, and re-layouts  9.11 us

profile of v1, /device:TPU:0, one launch (start us, length us, event | category | flops | bytes accessed | tf_op | source)
XLA Modules:
  0.0 33.6 jit_solution(3222913684849018301)
XLA Ops:
  0.0 0.0 copy-start.10
  0.0 0.0 copy-start.9
  0.0 0.0 copy-start.8
  0.0 0.8 %copy.13.w_task = bf16[128,8]{1,0:T(8,128)(2,1)S(1)} copy(bf16[128,8]{0,1:T(8,128)(2,1)} %param.22) | data formatting | bytes 4096 | tf_op args[10]
  0.8 0.0 copy-done.10
  0.8 0.0 copy-done.9
  0.9 0.0 copy-done.8
  0.9 0.0 copy-start
  0.9 1.0 %copy-done = bf16[384,512]{1,0:T(8,128)(2,1)S(1)} copy-done((bf16[384,512]{1,0:T(8,128)(2,1)S(1)}, bf16[384,512]{1,0:T(8,128)(2,1)}, u32[]{:S(2)}) %copy-start) | copy-done | bytes 393240
  1.9 0.0 copy-start.1
  1.9 0.9 %copy-done.1 = bf16[512,256]{1,0:T(8,128)(2,1)S(1)} copy-done((bf16[512,256]{1,0:T(8,128)(2,1)S(1)}, bf16[512,256]{1,0:T(8,128)(2,1)}, u32[]{:S(2)}) %copy-start.1) | copy-done | bytes 262168
  2.8 0.0 copy-start.2
  2.8 0.9 %copy-done.2 = bf16[512,256]{1,0:T(8,128)(2,1)S(1)} copy-done((bf16[512,256]{1,0:T(8,128)(2,1)S(1)}, bf16[512,256]{1,0:T(8,128)(2,1)}, u32[]{:S(2)}) %copy-start.2) | copy-done | bytes 262168
  3.8 0.0 copy-start.3
  3.8 0.9 %copy-done.3 = bf16[8,32,256]{2,1,0:T(8,128)(2,1)S(1)} copy-done((bf16[8,32,256]{2,1,0:T(8,128)(2,1)S(1)}, bf16[8,32,256]{2,1,0:T(8,128)(2,1)}, u32[]{:S(2)}) %copy-start.3) | copy-done | bytes 131096
  4.7 0.0 copy-start.4
  4.7 0.9 %copy-done.4 = bf16[256,256]{1,0:T(8,128)(2,1)S(1)} copy-done((bf16[256,256]{1,0:T(8,128)(2,1)S(1)}, bf16[256,256]{1,0:T(8,128)(2,1)}, u32[]{:S(2)}) %copy-start.4) | copy-done | bytes 131096
  5.6 0.0 copy-start.5
  5.6 0.9 %copy-done.5 = bf16[256,256]{1,0:T(8,128)(2,1)S(1)} copy-done((bf16[256,256]{1,0:T(8,128)(2,1)S(1)}, bf16[256,256]{1,0:T(8,128)(2,1)}, u32[]{:S(2)}) %copy-start.5) | copy-done | bytes 131096
  6.5 0.0 copy-start.6
  6.5 0.8 %copy-done.6 = bf16[256,128]{1,0:T(8,128)(2,1)S(1)} copy-done((bf16[256,128]{1,0:T(8,128)(2,1)S(1)}, bf16[256,128]{1,0:T(8,128)(2,1)}, u32[]{:S(2)}) %copy-start.6) | copy-done | bytes 65560
  7.3 0.0 copy-start.7
  7.3 0.8 %copy-done.7 = bf16[256,128]{1,0:T(8,128)(2,1)S(1)} copy-done((bf16[256,128]{1,0:T(8,128)(2,1)S(1)}, bf16[256,128]{1,0:T(8,128)(2,1)}, u32[]{:S(2)}) %copy-start.7) | copy-done | bytes 65560
  8.2 23.7 %score_users.1 = bf16[4,2,32,384]{3,2,1,0:T(8,128)(2,1)S(1)} custom-call(bf16[8,32,256]{2,1,0:T(8,128)(2,1)S(1)} %copy-done.3, s32[8]{0:T(128)S(1)} %copy-done.8, bf16[384,512]{1,0:T(8,128)(2,1)S(1)} %copy-done, bf16[512,256]{1,0:T(8,128)(2,1)S(1)} %copy-done.1, bf16[512,256]{1,0:T(8,128)(2,1)S(1)} %copy-done.2, bf16[256,256]{1,0:T(8,128)(2,1)S(1)} %copy-done.4, ...), custom_call_target="tpu_custom_call" | custom-call | tf_op jit(solution)/shard_map/score_users/pallas_call | solution.py:213
  32.0 0.0 copy-start.11
  32.1 0.9 %copy-done.11 = f32[8,9,8,384]{3,2,1,0:T(8,128)} copy-done((f32[8,9,8,384]{3,2,1,0:T(8,128)}, f32[8,9,8,384]{3,2,1,0:T(8,128)S(1)}, u32[]{:S(2)}) %copy-start.11) | copy-done | bytes 884760
  33.0 0.6 %constant_dynamic-update-slice_fusion = f32[8,9,8,384]{3,2,1,0:T(8,128)} fusion(f32[8,9,8,384]{3,2,1,0:T(8,128)} %copy-done.11, f32[8,1,8,384]{3,2,1,0:T(8,128)S(1)} %bitcast.14), kind=kLoop, calls=%fused_computation | loop fusion | bytes 196608 | tf_op jit(solution)/shard_map/stack | solution.py:241
  (9 shorter events, 0.1 us)
Async XLA Ops:
  0.0 0.8 %copy-start.10 = (f32[8]{0:T(128)S(1)}, f32[8]{0:T(128)}, u32[]{:S(2)}) copy-start(f32[8]{0:T(128)} %bias_task.1) | copy-start | bytes 100
  0.0 0.8 %copy-start.9 = (f32[128]{0:T(128)S(1)}, f32[128]{0:T(128)}, u32[]{:S(2)}) copy-start(f32[128]{0:T(128)} %bias_hidden.1) | copy-start | bytes 1540
  0.0 0.9 %copy-start.8 = (s32[8]{0:T(128)S(1)}, s32[8]{0:T(128)}, u32[]{:S(2)}) copy-start(s32[8]{0:T(128)} %lens.1) | copy-start | bytes 100
  0.9 1.0 %copy-start = (bf16[384,512]{1,0:T(8,128)(2,1)S(1)}, bf16[384,512]{1,0:T(8,128)(2,1)}, u32[]{:S(2)}) copy-start(bf16[384,512]{1,0:T(8,128)(2,1)} %items.1) | copy-start | bytes 1179652
  1.9 0.9 %copy-start.1 = (bf16[512,256]{1,0:T(8,128)(2,1)S(1)}, bf16[512,256]{1,0:T(8,128)(2,1)}, u32[]{:S(2)}) copy-start(bf16[512,256]{1,0:T(8,128)(2,1)} %w_query.1) | copy-start | bytes 786436
  2.8 0.9 %copy-start.2 = (bf16[512,256]{1,0:T(8,128)(2,1)S(1)}, bf16[512,256]{1,0:T(8,128)(2,1)}, u32[]{:S(2)}) copy-start(bf16[512,256]{1,0:T(8,128)(2,1)} %w_item.1) | copy-start | bytes 786436
  3.8 0.9 %copy-start.3 = (bf16[8,32,256]{2,1,0:T(8,128)(2,1)S(1)}, bf16[8,32,256]{2,1,0:T(8,128)(2,1)}, u32[]{:S(2)}) copy-start(bf16[8,32,256]{2,1,0:T(8,128)(2,1)} %hist.1) | copy-start | bytes 393220
  4.7 0.9 %copy-start.4 = (bf16[256,256]{1,0:T(8,128)(2,1)S(1)}, bf16[256,256]{1,0:T(8,128)(2,1)}, u32[]{:S(2)}) copy-start(bf16[256,256]{1,0:T(8,128)(2,1)} %w_key.1) | copy-start | bytes 393220
  5.6 0.9 %copy-start.5 = (bf16[256,256]{1,0:T(8,128)(2,1)S(1)}, bf16[256,256]{1,0:T(8,128)(2,1)}, u32[]{:S(2)}) copy-start(bf16[256,256]{1,0:T(8,128)(2,1)} %w_value.1) | copy-start | bytes 393220
  6.5 0.8 %copy-start.6 = (bf16[256,128]{1,0:T(8,128)(2,1)S(1)}, bf16[256,128]{1,0:T(8,128)(2,1)}, u32[]{:S(2)}) copy-start(bf16[256,128]{1,0:T(8,128)(2,1)} %w_pooled.1) | copy-start | bytes 196612
  7.3 0.8 %copy-start.7 = (bf16[256,128]{1,0:T(8,128)(2,1)S(1)}, bf16[256,128]{1,0:T(8,128)(2,1)}, u32[]{:S(2)}) copy-start(bf16[256,128]{1,0:T(8,128)(2,1)} %w_joint.1) | copy-start | bytes 196612
  32.0 0.9 %copy-start.11 = (f32[8,9,8,384]{3,2,1,0:T(8,128)}, f32[8,9,8,384]{3,2,1,0:T(8,128)S(1)}, u32[]{:S(2)}) copy-start(f32[8,9,8,384]{3,2,1,0:T(8,128)S(1)} %constant_dynamic-update-slice_fusion.1) | copy-start | bytes 2654212

commit v2 on v1

v2 whole, which is shorter than its diff:
```python
import functools
import math

import jax
import jax.numpy as jnp
from jax import lax
from jax.experimental import pallas as pl
from jax.experimental.pallas import tpu as pltpu
from jax.sharding import PartitionSpec as P

REACH = 4
WIN = 2 * REACH + 1
LEN_ROWS = 16
VMEM_BYTES = 64 * 1024 * 1024
F32, BF16 = jnp.float32, jnp.bfloat16


def offsets_of(n_blk):
    if n_blk >= WIN:
        return [k - REACH for k in range(WIN)], list(range(WIN))
    return list(range(n_blk)), [(k - REACH) % n_blk for k in range(WIN)]


def mm(a, b, dims=((1,), (0,))):
    return lax.dot_general(a, b, (dims, ((), ())), preferred_element_type=F32)


def partner_offsets(n_blk):
    if n_blk >= WIN:
        near = [0] + [sign * d for d in range(1, REACH + 1) for sign in (1, -1)]
        return [near] * n_blk
    return [
        [(m - g) % n_blk for g in sorted(range(n_blk), key=lambda g: (abs(g - m), g))]
        for m in range(n_blk)
    ]


def kernel(
    n_blk, n_x, n_sub, lens, bias_task, hist, *rest
):
    hbm, (out, tokens, *rest) = rest[:9], rest[9:]
    vmem, (projected, queries, terms, results, *sems) = rest[:9], rest[9:]
    z_send, z_recv, x_send, x_recv, c_send, c_recv, r_send, r_recv, load, load_tokens = sems
    items, w_query, w_item, w_joint, bias_hidden, w_key, w_value, w_pooled, w_task = vmem
    n_slots = out.shape[0]
    table = partner_offsets(n_blk)
    lowest = REACH if n_blk >= WIN else 0
    width = hist.shape[1]
    rows = hist.shape[0] // n_sub
    n_task, n_hid = w_task.shape
    count = results.shape[2] // n_task
    held = rows // count
    n_items = items.shape[0]
    all_items = n_sub * n_items
    me, x, c = lax.axis_index("blk"), lax.axis_index("users"), lax.axis_index("sub")

    def offset_at(step):
        found = jnp.int32(0)
        if n_blk >= WIN:
            for i, o in enumerate(table[0]):
                found = jnp.where(step == i, o, found)
        else:
            for m in range(n_blk):
                for i, o in enumerate(table[m]):
                    found = jnp.where((me == m) & (step == i), o, found)
        return found

    def slot_of(o):
        return o + lowest

    def mirror_of(o):
        return REACH - o if n_blk >= WIN else lax.rem(n_blk - o, n_blk)

    def partner_of(o):
        return lax.rem(me - o + n_blk, n_blk)

    def x_at(distance):
        return lax.rem(x + distance % n_x, n_x)

    def sub_at(distance):
        return lax.rem(c + distance % n_sub, n_sub)

    own = lowest
    own_tokens = pltpu.make_async_copy(
        hist.at[pl.ds(c * rows, rows)], tokens.at[own, x, pl.ds(0, rows)], load_tokens
    )
    own_tokens.start()
    loads = [pltpu.make_async_copy(a, b, load.at[i]) for i, (a, b) in enumerate(zip(hbm, vmem))]
    for copy in loads:
        copy.start()

    barrier = pltpu.get_barrier_semaphore()
    greeted = 0
    for o in range(-REACH, REACH + 1) if n_blk >= WIN else range(n_blk):
        for j in range(n_sub):
            if o != 0 or j != 0:
                target = {"blk": lax.rem(me + o % n_blk, n_blk), "sub": sub_at(j)}
                pl.semaphore_signal(barrier, inc=1, device_id=target)
                greeted += 1
    for j in range(1, n_x):
        pl.semaphore_signal(barrier, inc=1, device_id={"users": x_at(j)})
        greeted += 1

    row = lax.broadcasted_iota(jnp.int32, (LEN_ROWS, width), 0)
    length_rows = jnp.zeros((LEN_ROWS, width), F32)
    for u in range(count):
        length_rows = jnp.where(row == u, lens[c * count + u].astype(F32), length_rows)
    tokens[own, x, rows:, :] = length_rows.astype(BF16)
    own_tokens.wait()
    pl.semaphore_wait(barrier, greeted)

    def along_blk(o):
        return pltpu.make_async_remote_copy(
            tokens.at[own, x], tokens.at[mirror_of(o), x],
            z_send.at[mirror_of(o)], z_recv.at[mirror_of(o)],
            device_id={"blk": partner_of(o)},
        )

    def from_blk(o):
        there = tokens.at[slot_of(o), x]
        return pltpu.make_async_remote_copy(
            there, there, z_send.at[slot_of(o)], z_recv.at[slot_of(o)],
            device_id={"blk": partner_of(o)},
        )

    def along_x(s, j):
        return pltpu.make_async_remote_copy(
            tokens.at[s, x], tokens.at[s, x], x_send.at[s, j], x_recv.at[s, j],
            device_id={"users": x_at(j)},
        )

    def from_x(s, j):
        there = tokens.at[s, x_at(-j)]
        return pltpu.make_async_remote_copy(
            there, there, x_send.at[s, j], x_recv.at[s, j], device_id={"users": x_at(j)}
        )

    def along_sub(j):
        return pltpu.make_async_remote_copy(
            projected.at[c], projected.at[c], c_send.at[j], c_recv.at[j],
            device_id={"sub": sub_at(j)},
        )

    def from_sub(j):
        there = projected.at[sub_at(-j)]
        return pltpu.make_async_remote_copy(
            there, there, c_send.at[j], c_recv.at[j], device_id={"sub": sub_at(j)}
        )

    def back(o, j):
        s = slot_of(o)
        return pltpu.make_async_remote_copy(
            results.at[s, sub_at(j)], out.at[s, c], r_send.at[s, j], r_recv.at[s, j],
            device_id={"blk": partner_of(o), "sub": sub_at(j)},
        )

    def from_back(o, j):
        s = slot_of(o)
        there = out.at[s, sub_at(-j)]
        return pltpu.make_async_remote_copy(
            there, there, r_send.at[s, j], r_recv.at[s, j],
            device_id={"blk": partner_of(o), "sub": sub_at(j)},
        )

    own_back = pltpu.make_async_copy(results.at[own, c], out.at[own, c], r_send.at[own, 0])

    for j in range(1, n_x):
        along_x(own, j).start()
    for step in range(1, n_slots):
        along_blk(offset_at(step)).start()

    for copy in loads[:5]:
        copy.wait()
    item_rows = items[...]
    joined = mm(item_rows, w_item[...]).astype(BF16)
    projected[c, width:, :] = (mm(joined, w_joint[...]) + bias_hidden[...]).T.astype(BF16)
    projected[c, :width, :] = mm(item_rows, w_query[...]).T.astype(BF16)
    for j in range(1, n_sub):
        along_sub(j).start()

    for copy in loads[5:]:
        copy.wait()
    head = w_task[...].astype(F32)
    nothing = jnp.zeros_like(head)
    heads = jnp.concatenate(
        [jnp.concatenate([head, nothing], 1), jnp.concatenate([nothing, head], 1)], 0
    ).astype(BF16)
    row = lax.broadcasted_iota(jnp.int32, (2 * n_task, n_items), 0)
    bias = jnp.zeros((2 * n_task, n_items), F32)
    for t in range(n_task):
        bias = jnp.where((row == t) | (row == t + n_task), bias_task[t], bias)

    for j in range(1, n_sub):
        from_sub(j).wait_recv()
    for j in range(n_sub):
        queries[:, j * n_items : (j + 1) * n_items] = projected[j, :width, :]
        terms[:, j * n_items : (j + 1) * n_items] = projected[j, width:, :].astype(F32)

    factor = math.log2(math.e) / math.sqrt(width)
    place = lax.broadcasted_iota(jnp.int32, (n_x * held, 128), 0).astype(F32)

    def score(s):
        block = tokens[s, :, :rows, :].reshape(n_x * rows, width)
        keys = mm(block, w_key[...]).astype(BF16)
        values = mm(block, w_value[...]).astype(BF16)
        pooled_values = mm(values, w_pooled[...]).astype(BF16)
        valid_count = tokens[s, 0, rows:, :128].astype(F32)
        all_scores = mm(keys, queries[...])

        def of_user(array, u):
            return jnp.concatenate(
                [array[p * rows + u * held : p * rows + (u + 1) * held] for p in range(n_x)], 0
            )

        for first in range(0, count, 2):
            hidden = []
            for u in (first, first + 1):
                left_out = jnp.where(place < valid_count[u : u + 1], 0.0, -jnp.inf)
                scores = of_user(all_scores, u) + jnp.concatenate(
                    [left_out] * (all_items // 128), 1
                )
                expo = jnp.exp2((scores - jnp.max(scores, 0, keepdims=True)) * factor)
                weights = (expo * (1.0 / jnp.sum(expo, 0, keepdims=True))).astype(BF16)
                layer = mm(of_user(pooled_values, u), weights, ((0,), (0,))) + terms[...]
                hidden.append(jnp.maximum(layer.astype(BF16), jnp.zeros((), BF16)))
            logits = mm(heads, jnp.concatenate(hidden, 0))
            for j in range(n_sub):
                results[s, j, first * n_task : (first + 2) * n_task, :] = (
                    logits[:, j * n_items : (j + 1) * n_items] + bias
                ).astype(BF16)

    def one_step(step, carry):
        o = offset_at(step)
        s = slot_of(o)

        @pl.when(step + 1 < n_slots)
        def _():
            later = offset_at(step + 1)
            from_blk(later).wait_recv()
            for j in range(1, n_x):
                along_x(slot_of(later), j).start()

        for j in range(1, n_x):
            from_x(s, j).wait_recv()
        score(s)
        for j in range(1, n_sub):
            back(o, j).start()

        @pl.when(step == 0)
        def _():
            own_back.start()

        @pl.when(step > 0)
        def _():
            back(o, 0).start()

        return carry

    lax.fori_loop(0, n_slots, one_step, jnp.int32(0))

    own_back.wait()
    for step in range(n_slots):
        o = offset_at(step)
        if step > 0:
            along_blk(o).wait_send()
        for j in range(1, n_x):
            along_x(slot_of(o), j).wait_send()
        for j in range(0 if step > 0 else 1, n_sub):
            back(o, j).wait_send()
    for s in range(n_slots):
        o = s - lowest
        for j in range(0 if s != own else 1, n_sub):
            from_back(o, j).wait_recv()
    for j in range(1, n_sub):
        along_sub(j).wait_send()


def spread(place_of, by_slot, out, near, wide, load, sems):
    copies = []
    n_slots = by_slot.shape[0]
    loads = [pltpu.make_async_copy(by_slot.at[s], near.at[s], load.at[s]) for s in range(n_slots)]
    for copy in loads:
        copy.start()
    for s in range(n_slots):
        loads[s].wait()
        wide[s] = near[s].astype(F32).reshape(wide.shape[1:])
        for k, slot in enumerate(place_of):
            if slot == s:
                copies.append(pltpu.make_async_copy(wide.at[s], out.at[:, k], sems.at[k]))
                copies[-1].start()
    for copy in copies:
        copy.wait()


def shards(
    n_blk, n_x, n_sub, history, lengths, item_rows, w_query, w_item, w_key, w_value, w_pooled,
    w_joint, bias_hidden, w_task, bias_task,
):
    offsets, place_of = offsets_of(n_blk)
    users, held, width = history.shape
    n_items = item_rows.shape[0]
    n_hid, n_task = w_task.shape
    n_slots, count = len(offsets), users // n_sub
    hbm, smem = pl.BlockSpec(memory_space=pltpu.HBM), pl.BlockSpec(memory_space=pltpu.SMEM)
    dma = pltpu.SemaphoreType.DMA
    held_here = (
        item_rows, w_query, w_item, w_joint, bias_hidden[None], w_key, w_value, w_pooled, w_task.T,
    )
    by_slot = pl.pallas_call(
        functools.partial(kernel, n_blk, n_x, n_sub),
        out_shape=jax.ShapeDtypeStruct((n_slots, n_sub, count * n_task, n_items), BF16),
        in_specs=[smem, smem, hbm] + [hbm] * len(held_here),
        out_specs=pl.BlockSpec(memory_space=pl.ANY),
        scratch_shapes=[
            pltpu.VMEM((n_slots, n_x, count * held + LEN_ROWS, width), BF16),
            *[pltpu.VMEM(a.shape, a.dtype) for a in held_here],
            pltpu.VMEM((n_sub, width + n_hid, n_items), BF16),
            pltpu.VMEM((width, n_sub * n_items), BF16),
            pltpu.VMEM((n_hid, n_sub * n_items), F32),
            pltpu.VMEM((n_slots, n_sub, count * n_task, n_items), BF16),
            dma((n_slots,)),
            dma((n_slots,)),
            dma((n_slots, n_x)),
            dma((n_slots, n_x)),
            dma((n_sub,)),
            dma((n_sub,)),
            dma((n_slots, n_sub)),
            dma((n_slots, n_sub)),
            dma((len(held_here),)),
            dma,
        ],
        compiler_params=pltpu.CompilerParams(
            collective_id=0, has_side_effects=True, vmem_limit_bytes=VMEM_BYTES
        ),
        name="score_users",
    )(lengths, bias_task, history.reshape(users * held, width), *held_here)
    return pl.pallas_call(
        functools.partial(spread, place_of),
        out_shape=jax.ShapeDtypeStruct((users, WIN, n_task, n_items), F32),
        in_specs=[hbm],
        out_specs=pl.BlockSpec(memory_space=pltpu.HBM),
        scratch_shapes=[
            pltpu.VMEM(by_slot.shape, BF16),
            pltpu.VMEM((n_slots, users, n_task, n_items), F32),
            dma((n_slots,)),
            dma((WIN,)),
        ],
        compiler_params=pltpu.CompilerParams(vmem_limit_bytes=VMEM_BYTES),
        name="spread",
    )(by_slot)


def solution(mesh):
    placed = (
        P(("parts", "blk"), "users", None),
        P(("parts", "blk")),
        P(("parts", "blk", "users", "sub"), None),
    ) + (P(),) * 9
    sizes = (mesh.shape["blk"], mesh.shape["users"], mesh.shape["sub"])
    return jax.shard_map(
        functools.partial(shards, *sizes),
        mesh=mesh,
        in_specs=placed,
        out_specs=P(("parts", "blk"), None, None, ("users", "sub")),
        check_vma=False,
    )
```

time: 34.1 us -> 27.5 us (0.81)
  local copies, waits for them, and re-layouts: 9.79 us -> 0 us
  Pallas kernels: 23.7 us -> 27.3 us
    unnamed x33 -> x0, local copies, waits for them, and re-layouts: 9.11 us -> none
    pallas_call x0 -> x1, Pallas kernels: none -> 1.82 us  [shards(): pl.pallas_call(functools.partial(spread, place_of), out_shape=jax.ShapeDt...]
    pallas_call x1, Pallas kernels: 23.7 us -> 25.5 us  [shards(): pl.pallas_call(functools.partial(kernel, n_blk, n_x, n_sub), out_shape=ja...]
    another operation x1 -> x0, local copies, waits for them, and re-layouts: 0.65 us -> none  [shards(): return jnp.stack([by_offset[s] for s in place_of], axis=1)]
where the time goes in v2:
time: 27.5 us; the launch traced here: 27.3 us
  Pallas kernels  27.3 us (99%)
    pallas_call x1, Pallas kernels, shards(): pl.pallas_call(functools.partial(kernel, n_blk, n_x, n_sub), out_shape=ja...  25.5 us
    pallas_call x1, Pallas kernels, shards(): pl.pallas_call(functools.partial(spread, place_of), out_shape=jax.ShapeDt...  1.82 us

profile of v2, /device:TPU:0, one launch (start us, length us, event | category | flops | bytes accessed | tf_op | source)
XLA Modules:
  0.0 27.3 jit_solution(1778969216642041870)
XLA Ops:
  0.0 25.5 %score_users.1.by_slot = bf16[4,2,32,384]{3,2,1,0:T(8,128)(2,1)} custom-call(s32[8]{0:T(128)} %lens.1, f32[8]{0:T(128)} %bias_task.1, bf16[256,256]{1,0:T(8,128)(2,1)} %bitcast.3, bf16[384,512]{1,0:T(8,128)(2,1)} %rest_0_.1, bf16[512,256]{1,0:T(8,128)(2,1)} %rest_1_.1, bf16[512,256]{1,0:T(8,128)(2,1)} %rest_2_.1, bf16[256,128]{1,0:T(8,128)(2,1)} %rest_3_.1, ...), custom_call_target="tpu_custom_call" | custom-call | tf_op jit(solution)/shard_map/score_users/pallas_call | solution.py:309
  25.5 1.8 %spread.1 = f32[8,9,8,384]{3,2,1,0:T(8,128)} custom-call(bf16[4,2,32,384]{3,2,1,0:T(8,128)(2,1)} %score_users.1.by_slot), custom_call_target="tpu_custom_call" | custom-call | tf_op jit(solution)/shard_map/spread/pallas_call | solution.py:337

commit v3 on v2

--- a/solution.py
+++ b/solution.py
@@ -10,7 +10,7 @@
 
 REACH = 4
 WIN = 2 * REACH + 1
-LEN_ROWS = 16
+LEFT_OUT = 1024.0
 VMEM_BYTES = 64 * 1024 * 1024
 F32, BF16 = jnp.float32, jnp.bfloat16
 
@@ -82,7 +82,7 @@
 
     own = lowest
     own_tokens = pltpu.make_async_copy(
-        hist.at[pl.ds(c * rows, rows)], tokens.at[own, x, pl.ds(0, rows)], load_tokens
+        hist.at[pl.ds(c * rows, rows)], tokens.at[own, x], load_tokens
     )
     own_tokens.start()
     loads = [pltpu.make_async_copy(a, b, load.at[i]) for i, (a, b) in enumerate(zip(hbm, vmem))]
@@ -101,12 +101,12 @@
         pl.semaphore_signal(barrier, inc=1, device_id={"users": x_at(j)})
         greeted += 1
 
-    row = lax.broadcasted_iota(jnp.int32, (LEN_ROWS, width), 0)
-    length_rows = jnp.zeros((LEN_ROWS, width), F32)
+    own_tokens.wait()
+    row = lax.broadcasted_iota(jnp.int32, (held, width), 0) + x * held
     for u in range(count):
-        length_rows = jnp.where(row == u, lens[c * count + u].astype(F32), length_rows)
-    tokens[own, x, rows:, :] = length_rows.astype(BF16)
-    own_tokens.wait()
+        mine = tokens[own, x, u * held : (u + 1) * held, :]
+        marked = jnp.where(row < lens[c * count + u], mine.astype(F32), LEFT_OUT)
+        tokens[own, x, u * held : (u + 1) * held, :] = marked.astype(BF16)
     pl.semaphore_wait(barrier, greeted)
 
     def along_blk(o):
@@ -183,12 +183,17 @@
     head = w_task[...].astype(F32)
     nothing = jnp.zeros_like(head)
     heads = jnp.concatenate(
-        [jnp.concatenate([head, nothing], 1), jnp.concatenate([nothing, head], 1)], 0
+        [
+            jnp.concatenate([head if v == u else nothing for v in range(count)], 1)
+            for u in range(count)
+        ],
+        0,
     ).astype(BF16)
-    row = lax.broadcasted_iota(jnp.int32, (2 * n_task, n_items), 0)
-    bias = jnp.zeros((2 * n_task, n_items), F32)
+    row = lax.rem(lax.broadcasted_iota(jnp.int32, (count * n_task, 128), 0), n_task)
+    bias = jnp.zeros((count * n_task, 128), F32)
     for t in range(n_task):
-        bias = jnp.where((row == t) | (row == t + n_task), bias_task[t], bias)
+        bias = jnp.where(row == t, bias_task[t], bias)
+    user = lax.rem(lax.broadcasted_iota(jnp.int32, (n_hid, n_x * rows), 1) // held, count)
 
     for j in range(1, n_sub):
         from_sub(j).wait_recv()
@@ -197,37 +202,42 @@
         terms[:, j * n_items : (j + 1) * n_items] = projected[j, width:, :].astype(F32)
 
     factor = math.log2(math.e) / math.sqrt(width)
-    place = lax.broadcasted_iota(jnp.int32, (n_x * held, 128), 0).astype(F32)
+    lanes = 256 if all_items % 256 == 0 else 128
 
     def score(s):
-        block = tokens[s, :, :rows, :].reshape(n_x * rows, width)
+        block = tokens[s].reshape(n_x * rows, width)
         keys = mm(block, w_key[...]).astype(BF16)
         values = mm(block, w_value[...]).astype(BF16)
-        pooled_values = mm(values, w_pooled[...]).astype(BF16)
-        valid_count = tokens[s, 0, rows:, :128].astype(F32)
-        all_scores = mm(keys, queries[...])
-
-        def of_user(array, u):
-            return jnp.concatenate(
-                [array[p * rows + u * held : p * rows + (u + 1) * held] for p in range(n_x)], 0
-            )
-
-        for first in range(0, count, 2):
-            hidden = []
-            for u in (first, first + 1):
-                left_out = jnp.where(place < valid_count[u : u + 1], 0.0, -jnp.inf)
-                scores = of_user(all_scores, u) + jnp.concatenate(
-                    [left_out] * (all_items // 128), 1
+        pooled_values = mm(values, w_pooled[...]).T
+        by_user = jnp.concatenate(
+            [jnp.where(user == u, pooled_values, 0.0).astype(BF16) for u in range(count)], 0
+        )
+        left_out = jnp.where(block[:, :128].astype(F32) > LEFT_OUT / 2, -jnp.inf, 0.0)
+
+        def pieces(array, u):
+            at = [p * rows + u * held for p in range(n_x)]
+            return jnp.concatenate([array[i : i + held] for i in at], 0)
+
+        for low in range(0, all_items, lanes):
+            all_scores = mm(keys, queries[:, low : low + lanes])
+            weights = []
+            for u in range(count):
+                scores = pieces(all_scores, u) + jnp.concatenate(
+                    [pieces(left_out, u)] * (lanes // 128), 1
                 )
                 expo = jnp.exp2((scores - jnp.max(scores, 0, keepdims=True)) * factor)
-                weights = (expo * (1.0 / jnp.sum(expo, 0, keepdims=True))).astype(BF16)
-                layer = mm(of_user(pooled_values, u), weights, ((0,), (0,))) + terms[...]
-                hidden.append(jnp.maximum(layer.astype(BF16), jnp.zeros((), BF16)))
-            logits = mm(heads, jnp.concatenate(hidden, 0))
-            for j in range(n_sub):
-                results[s, j, first * n_task : (first + 2) * n_task, :] = (
-                    logits[:, j * n_items : (j + 1) * n_items] + bias
-                ).astype(BF16)
+                weights.append((expo * (1.0 / jnp.sum(expo, 0, keepdims=True))).astype(BF16))
+            weights = jnp.concatenate(
+                [w[p * held : (p + 1) * held] for p in range(n_x) for w in weights], 0
+            )
+            layer = mm(by_user, weights) + jnp.concatenate(
+                [terms[:, low : low + lanes]] * count, 0
+            )
+            hidden = jnp.maximum(layer.astype(BF16), jnp.zeros((), BF16))
+            logits = mm(heads, hidden)
+            for i in range(0, lanes, 128):
+                j, at = divmod(low + i, n_items)
+                results[s, j, :, at : at + 128] = (logits[:, i : i + 128] + bias).astype(BF16)
 
     def one_step(step, carry):
         o = offset_at(step)
@@ -312,7 +322,7 @@
         in_specs=[smem, smem, hbm] + [hbm] * len(held_here),
         out_specs=pl.BlockSpec(memory_space=pl.ANY),
         scratch_shapes=[
-            pltpu.VMEM((n_slots, n_x, count * held + LEN_ROWS, width), BF16),
+            pltpu.VMEM((n_slots, n_x, count * held, width), BF16),
             *[pltpu.VMEM(a.shape, a.dtype) for a in held_here],
             pltpu.VMEM((n_sub, width + n_hid, n_items), BF16),
             pltpu.VMEM((width, n_sub * n_items), BF16),

time: 27.5 us -> 27.6 us (level)
  no operation moved by 1% of the time
where the time goes in v3:
time: 27.6 us; the launch traced here: 27.4 us
  Pallas kernels  27.4 us (99%)
    pallas_call x1, Pallas kernels, shards(): pl.pallas_call(functools.partial(kernel, n_blk, n_x, n_sub), out_shape=ja...  25.6 us
    pallas_call x1, Pallas kernels, shards(): pl.pallas_call(functools.partial(spread, place_of), out_shape=jax.ShapeDt...  1.82 us

profile of v3, /device:TPU:0, one launch (start us, length us, event | category | flops | bytes accessed | tf_op | source)
XLA Modules:
  0.0 27.4 jit_solution(3780343070727213667)
XLA Ops:
  0.0 25.6 %score_users.1.by_slot = bf16[4,2,32,384]{3,2,1,0:T(8,128)(2,1)} custom-call(s32[8]{0:T(128)} %lens.1, f32[8]{0:T(128)} %bias_task.1, bf16[256,256]{1,0:T(8,128)(2,1)} %bitcast.3, bf16[384,512]{1,0:T(8,128)(2,1)} %rest_0_.1, bf16[512,256]{1,0:T(8,128)(2,1)} %rest_1_.1, bf16[512,256]{1,0:T(8,128)(2,1)} %rest_2_.1, bf16[256,128]{1,0:T(8,128)(2,1)} %rest_3_.1, ...), custom_call_target="tpu_custom_call" | custom-call | tf_op jit(solution)/shard_map/score_users/pallas_call | solution.py:319
  25.6 1.8 %spread.1 = f32[8,9,8,384]{3,2,1,0:T(8,128)} custom-call(bf16[4,2,32,384]{3,2,1,0:T(8,128)(2,1)} %score_users.1.by_slot), custom_call_target="tpu_custom_call" | custom-call | tf_op jit(solution)/shard_map/spread/pallas_call | solution.py:347

commit v4 on v3

--- a/solution.py
+++ b/solution.py
@@ -10,6 +10,7 @@
 
 REACH = 4
 WIN = 2 * REACH + 1
+PAIRS = 2
 LEFT_OUT = 1024.0
 VMEM_BYTES = 64 * 1024 * 1024
 F32, BF16 = jnp.float32, jnp.bfloat16
@@ -25,14 +26,20 @@
     return lax.dot_general(a, b, (dims, ((), ())), preferred_element_type=F32)
 
 
-def partner_offsets(n_blk):
-    if n_blk >= WIN:
-        near = [0] + [sign * d for d in range(1, REACH + 1) for sign in (1, -1)]
-        return [near] * n_blk
-    return [
-        [(m - g) % n_blk for g in sorted(range(n_blk), key=lambda g: (abs(g - m), g))]
-        for m in range(n_blk)
-    ]
+def steps_of(n_blk):
+    ring = n_blk >= WIN
+    orders = []
+    for m in range(n_blk):
+        order = []
+        for d in range(REACH + 1 if ring else n_blk):
+            for q in range(PAIRS):
+                for g in [m] if d == 0 else [m - d, m + d]:
+                    if ring:
+                        order.append((m - g, q))
+                    elif 0 <= g < n_blk:
+                        order.append(((m - g) % n_blk, q))
+        orders.append(order)
+    return orders[:1] * n_blk if ring else orders
 
 
 def kernel(
@@ -40,37 +47,33 @@
 ):
     hbm, (out, tokens, *rest) = rest[:9], rest[9:]
     vmem, (projected, queries, terms, results, *sems) = rest[:9], rest[9:]
-    z_send, z_recv, x_send, x_recv, c_send, c_recv, r_send, r_recv, load, load_tokens = sems
+    own_send, z_send, z_recv, x_send, x_recv, c_send, c_recv, r_send, r_recv, load, load_tokens = sems
     items, w_query, w_item, w_joint, bias_hidden, w_key, w_value, w_pooled, w_task = vmem
     n_slots = out.shape[0]
-    table = partner_offsets(n_blk)
+    table = steps_of(n_blk)
+    n_steps = n_slots * PAIRS
+    ring = n_blk >= WIN
     lowest = REACH if n_blk >= WIN else 0
     width = hist.shape[1]
-    rows = hist.shape[0] // n_sub
+    rows = tokens.shape[3]
     n_task, n_hid = w_task.shape
-    count = results.shape[2] // n_task
+    count = results.shape[3] // n_task
     held = rows // count
     n_items = items.shape[0]
     all_items = n_sub * n_items
     me, x, c = lax.axis_index("blk"), lax.axis_index("users"), lax.axis_index("sub")
 
-    def offset_at(step):
-        found = jnp.int32(0)
-        if n_blk >= WIN:
-            for i, o in enumerate(table[0]):
-                found = jnp.where(step == i, o, found)
-        else:
-            for m in range(n_blk):
-                for i, o in enumerate(table[m]):
-                    found = jnp.where((me == m) & (step == i), o, found)
-        return found
+    def step_at(step):
+        o, q = jnp.int32(0), jnp.int32(0)
+        for m in range(1 if ring else n_blk):
+            for i, entry in enumerate(table[m]):
+                here = (step == i) if ring else (me == m) & (step == i)
+                o, q = jnp.where(here, entry[0], o), jnp.where(here, entry[1], q)
+        return o, q
 
     def slot_of(o):
         return o + lowest
 
-    def mirror_of(o):
-        return REACH - o if n_blk >= WIN else lax.rem(n_blk - o, n_blk)
-
     def partner_of(o):
         return lax.rem(me - o + n_blk, n_blk)
 
@@ -81,10 +84,14 @@
         return lax.rem(c + distance % n_sub, n_sub)
 
     own = lowest
-    own_tokens = pltpu.make_async_copy(
-        hist.at[pl.ds(c * rows, rows)], tokens.at[own, x], load_tokens
-    )
-    own_tokens.start()
+    own_tokens = [
+        pltpu.make_async_copy(
+            hist.at[pl.ds((c * PAIRS + q) * rows, rows)], tokens.at[own, q, x], load_tokens.at[q]
+        )
+        for q in range(PAIRS)
+    ]
+    for copy in own_tokens:
+        copy.start()
     loads = [pltpu.make_async_copy(a, b, load.at[i]) for i, (a, b) in enumerate(zip(hbm, vmem))]
     for copy in loads:
         copy.start()
@@ -101,39 +108,91 @@
         pl.semaphore_signal(barrier, inc=1, device_id={"users": x_at(j)})
         greeted += 1
 
-    own_tokens.wait()
     row = lax.broadcasted_iota(jnp.int32, (held, width), 0) + x * held
-    for u in range(count):
-        mine = tokens[own, x, u * held : (u + 1) * held, :]
-        marked = jnp.where(row < lens[c * count + u], mine.astype(F32), LEFT_OUT)
-        tokens[own, x, u * held : (u + 1) * held, :] = marked.astype(BF16)
+    for q in range(PAIRS):
+        own_tokens[q].wait()
+        for u in range(count):
+            mine = tokens[own, q, x, u * held : (u + 1) * held, :].astype(F32)
+            marked = jnp.where(row < lens[(c * PAIRS + q) * count + u], mine, LEFT_OUT)
+            tokens[own, q, x, u * held : (u + 1) * held, :] = marked.astype(BF16)
     pl.semaphore_wait(barrier, greeted)
 
-    def along_blk(o):
-        return pltpu.make_async_remote_copy(
-            tokens.at[own, x], tokens.at[mirror_of(o), x],
-            z_send.at[mirror_of(o)], z_recv.at[mirror_of(o)],
+    def beside(sign):
+        there = lax.rem(me + sign + n_blk, n_blk)
+        exists = None if ring else (me + 1 < n_blk if sign > 0 else me > 0)
+
+        def seen(o):
+            return o + sign + lowest if ring else lax.rem(o + sign + n_blk, n_blk)
+
+        return there, exists, seen
+
+    def own_along_blk(sign, q, act):
+        there, exists, seen = beside(sign)
+        side = 0 if sign > 0 else 1
+
+        def go():
+            act(
+                pltpu.make_async_remote_copy(
+                    tokens.at[own, q, x], tokens.at[seen(0), q, x],
+                    own_send.at[side, q], z_recv.at[seen(0), q], device_id={"blk": there},
+                )
+            )
+
+        if exists is None:
+            go()
+        else:
+            pl.when(exists)(go)
+
+    def relay(o, q, act):
+        s = slot_of(o)
+        for sign in (1, -1):
+            there, exists, seen = beside(sign)
+            if ring:
+                onward = (o > 0) & (o < REACH) if sign > 0 else (o < 0) & (o > -REACH)
+            else:
+                came = partner_of(o) < me if sign > 0 else partner_of(o) > me
+                onward = came & exists
+
+            @pl.when(onward)
+            def _():
+                act(
+                    pltpu.make_async_remote_copy(
+                        tokens.at[s, q, x], tokens.at[seen(o), q, x],
+                        z_send.at[s, q], z_recv.at[seen(o), q], device_id={"blk": there},
+                    )
+                )
+
+    def from_blk(o, q):
+        there = tokens.at[slot_of(o), q, x]
+        return pltpu.make_async_remote_copy(
+            there, there, z_send.at[slot_of(o), q], z_recv.at[slot_of(o), q],
             device_id={"blk": partner_of(o)},
         )
 
-    def from_blk(o):
-        there = tokens.at[slot_of(o), x]
-        return pltpu.make_async_remote_copy(
-            there, there, z_send.at[slot_of(o)], z_recv.at[slot_of(o)],
-            device_id={"blk": partner_of(o)},
-        )
-
-    def along_x(s, j):
-        return pltpu.make_async_remote_copy(
-            tokens.at[s, x], tokens.at[s, x], x_send.at[s, j], x_recv.at[s, j],
+    def along_x(s, q, j):
+        return pltpu.make_async_remote_copy(
+            tokens.at[s, q, x], tokens.at[s, q, x], x_send.at[s, q, j], x_recv.at[s, q, j],
             device_id={"users": x_at(j)},
         )
 
-    def from_x(s, j):
-        there = tokens.at[s, x_at(-j)]
-        return pltpu.make_async_remote_copy(
-            there, there, x_send.at[s, j], x_recv.at[s, j], device_id={"users": x_at(j)}
-        )
+    def from_x(s, q, j):
+        there = tokens.at[s, q, x_at(-j)]
+        return pltpu.make_async_remote_copy(
+            there, there, x_send.at[s, q, j], x_recv.at[s, q, j], device_id={"users": x_at(j)}
+        )
+
+    def start(copy):
+        copy.start()
+
+    def wait_send(copy):
+        copy.wait_send()
+
+    def hand_on(step):
+        o, q = step_at(step)
+        from_blk(o, q).wait_recv()
+        relay(o, q, start)
+        for j in range(1, n_x):
+            along_x(slot_of(o), q, j).start()
 
     def along_sub(j):
         return pltpu.make_async_remote_copy(
@@ -147,27 +206,31 @@
             there, there, c_send.at[j], c_recv.at[j], device_id={"sub": sub_at(j)}
         )
 
-    def back(o, j):
+    def back(o, q, j):
         s = slot_of(o)
         return pltpu.make_async_remote_copy(
-            results.at[s, sub_at(j)], out.at[s, c], r_send.at[s, j], r_recv.at[s, j],
+            results.at[s, q, sub_at(j)], out.at[s, c, q], r_send.at[s, q, j], r_recv.at[s, q, j],
             device_id={"blk": partner_of(o), "sub": sub_at(j)},
         )
 
-    def from_back(o, j):
+    def from_back(o, q, j):
         s = slot_of(o)
-        there = out.at[s, sub_at(-j)]
-        return pltpu.make_async_remote_copy(
-            there, there, r_send.at[s, j], r_recv.at[s, j],
+        there = out.at[s, sub_at(-j), q]
+        return pltpu.make_async_remote_copy(
+            there, there, r_send.at[s, q, j], r_recv.at[s, q, j],
             device_id={"blk": partner_of(o), "sub": sub_at(j)},
         )
 
-    own_back = pltpu.make_async_copy(results.at[own, c], out.at[own, c], r_send.at[own, 0])
-
-    for j in range(1, n_x):
-        along_x(own, j).start()
-    for step in range(1, n_slots):
-        along_blk(offset_at(step)).start()
+    def own_back(q):
+        return pltpu.make_async_copy(
+            results.at[own, q, c], out.at[own, c, q], r_send.at[own, q, 0]
+        )
+
+    for q in range(PAIRS):
+        for sign in (1, -1):
+            own_along_blk(sign, q, start)
+        for j in range(1, n_x):
+            along_x(own, q, j).start()
 
     for copy in loads[:5]:
         copy.wait()
@@ -177,6 +240,9 @@
     projected[c, :width, :] = mm(item_rows, w_query[...]).T.astype(BF16)
     for j in range(1, n_sub):
         along_sub(j).start()
+
+    for step in range(PAIRS, min(n_steps, PAIRS + 2)):
+        hand_on(step)
 
     for copy in loads[5:]:
         copy.wait()
@@ -204,8 +270,8 @@
     factor = math.log2(math.e) / math.sqrt(width)
     lanes = 256 if all_items % 256 == 0 else 128
 
-    def score(s):
-        block = tokens[s].reshape(n_x * rows, width)
+    def score(s, q):
+        block = tokens[s, q].reshape(n_x * rows, width)
         keys = mm(block, w_key[...]).astype(BF16)
         values = mm(block, w_value[...]).astype(BF16)
         pooled_values = mm(values, w_pooled[...]).T
@@ -237,50 +303,51 @@
             logits = mm(heads, hidden)
             for i in range(0, lanes, 128):
                 j, at = divmod(low + i, n_items)
-                results[s, j, :, at : at + 128] = (logits[:, i : i + 128] + bias).astype(BF16)
+                results[s, q, j, :, at : at + 128] = (logits[:, i : i + 128] + bias).astype(BF16)
 
     def one_step(step, carry):
-        o = offset_at(step)
+        o, q = step_at(step)
         s = slot_of(o)
-
-        @pl.when(step + 1 < n_slots)
+        ahead = jnp.where(step < 2, step + PAIRS + 2, step + PAIRS + 1)
+
+        @pl.when((step != 2) & (ahead < n_steps))
         def _():
-            later = offset_at(step + 1)
-            from_blk(later).wait_recv()
-            for j in range(1, n_x):
-                along_x(slot_of(later), j).start()
+            hand_on(ahead)
 
         for j in range(1, n_x):
-            from_x(s, j).wait_recv()
-        score(s)
+            from_x(s, q, j).wait_recv()
+        score(s, q)
         for j in range(1, n_sub):
-            back(o, j).start()
-
-        @pl.when(step == 0)
+            back(o, q, j).start()
+
+        @pl.when(step < PAIRS)
         def _():
-            own_back.start()
-
-        @pl.when(step > 0)
+            own_back(q).start()
+
+        @pl.when(step >= PAIRS)
         def _():
-            back(o, 0).start()
+            back(o, q, 0).start()
 
         return carry
 
-    lax.fori_loop(0, n_slots, one_step, jnp.int32(0))
-
-    own_back.wait()
-    for step in range(n_slots):
-        o = offset_at(step)
-        if step > 0:
-            along_blk(o).wait_send()
+    lax.fori_loop(0, n_steps, one_step, jnp.int32(0))
+
+    for q in range(PAIRS):
+        own_back(q).wait()
+        for sign in (1, -1):
+            own_along_blk(sign, q, wait_send)
+    for step in range(n_steps):
+        o, q = step_at(step)
+        if step >= PAIRS:
+            relay(o, q, wait_send)
         for j in range(1, n_x):
-            along_x(slot_of(o), j).wait_send()
-        for j in range(0 if step > 0 else 1, n_sub):
-            back(o, j).wait_send()
+            along_x(slot_of(o), q, j).wait_send()
+        for j in range(0 if step >= PAIRS else 1, n_sub):
+            back(o, q, j).wait_send()
     for s in range(n_slots):
-        o = s - lowest
-        for j in range(0 if s != own else 1, n_sub):
-            from_back(o, j).wait_recv()
+        for q in range(PAIRS):
+            for j in range(0 if s != own else 1, n_sub):
+                from_back(s - lowest, q, j).wait_recv()
     for j in range(1, n_sub):
         along_sub(j).wait_send()
 
@@ -310,7 +377,7 @@
     users, held, width = history.shape
     n_items = item_rows.shape[0]
     n_hid, n_task = w_task.shape
-    n_slots, count = len(offsets), users // n_sub
+    n_slots, count = len(offsets), users // n_sub // PAIRS
     hbm, smem = pl.BlockSpec(memory_space=pltpu.HBM), pl.BlockSpec(memory_space=pltpu.SMEM)
     dma = pltpu.SemaphoreType.DMA
     held_here = (
@@ -318,26 +385,27 @@
     )
     by_slot = pl.pallas_call(
         functools.partial(kernel, n_blk, n_x, n_sub),
-        out_shape=jax.ShapeDtypeStruct((n_slots, n_sub, count * n_task, n_items), BF16),
+        out_shape=jax.ShapeDtypeStruct((n_slots, n_sub, PAIRS, count * n_task, n_items), BF16),
         in_specs=[smem, smem, hbm] + [hbm] * len(held_here),
         out_specs=pl.BlockSpec(memory_space=pl.ANY),
         scratch_shapes=[
-            pltpu.VMEM((n_slots, n_x, count * held, width), BF16),
+            pltpu.VMEM((n_slots, PAIRS, n_x, count * held, width), BF16),
             *[pltpu.VMEM(a.shape, a.dtype) for a in held_here],
             pltpu.VMEM((n_sub, width + n_hid, n_items), BF16),
             pltpu.VMEM((width, n_sub * n_items), BF16),
             pltpu.VMEM((n_hid, n_sub * n_items), F32),
-            pltpu.VMEM((n_slots, n_sub, count * n_task, n_items), BF16),
-            dma((n_slots,)),
-            dma((n_slots,)),
-            dma((n_slots, n_x)),
-            dma((n_slots, n_x)),
+            pltpu.VMEM((n_slots, PAIRS, n_sub, count * n_task, n_items), BF16),
+            dma((2, PAIRS)),
+            dma((n_slots, PAIRS)),
+            dma((n_slots, PAIRS)),
+            dma((n_slots, PAIRS, n_x)),
+            dma((n_slots, PAIRS, n_x)),
             dma((n_sub,)),
             dma((n_sub,)),
-            dma((n_slots, n_sub)),
-            dma((n_slots, n_sub)),
+            dma((n_slots, PAIRS, n_sub)),
+            dma((n_slots, PAIRS, n_sub)),
             dma((len(held_here),)),
-            dma,
+            dma((PAIRS,)),
         ],
         compiler_params=pltpu.CompilerParams(
             collective_id=0, has_side_effects=True, vmem_limit_bytes=VMEM_BYTES

time: 27.6 us -> 29.7 us (1.076)
  Pallas kernels: 27.4 us -> 29.5 us
    pallas_call x1, Pallas kernels: 25.6 us -> 27.7 us  [shards(): pl.pallas_call(functools.partial(kernel, n_blk, n_x, n_sub), out_shape=ja...]
where the time goes in v4:
time: 29.7 us; the launch traced here: 29.5 us
  Pallas kernels  29.5 us (99%)
    pallas_call x1, Pallas kernels, shards(): pl.pallas_call(functools.partial(kernel, n_blk, n_x, n_sub), out_shape=ja...  27.7 us
    pallas_call x1, Pallas kernels, shards(): pl.pallas_call(functools.partial(spread, place_of), out_shape=jax.ShapeDt...  1.82 us

profile of v4, /device:TPU:0, one launch (start us, length us, event | category | flops | bytes accessed | tf_op | source)
XLA Modules:
  0.0 29.5 jit_solution(12487044650218567259)
XLA Ops:
  0.0 27.7 %score_users.1.by_slot = bf16[4,2,2,16,384]{4,3,2,1,0:T(8,128)(2,1)} custom-call(s32[8]{0:T(128)} %lens.1, f32[8]{0:T(128)} %bias_task.1, bf16[256,256]{1,0:T(8,128)(2,1)} %bitcast.3, bf16[384,512]{1,0:T(8,128)(2,1)} %rest_0_.1, bf16[512,256]{1,0:T(8,128)(2,1)} %rest_1_.1, bf16[512,256]{1,0:T(8,128)(2,1)} %rest_2_.1, bf16[256,128]{1,0:T(8,128)(2,1)} %rest_3_.1, ...), custom_call_target="tpu_custom_call" | custom-call | tf_op jit(solution)/shard_map/score_users/pallas_call | solution.py:386
  27.7 1.8 %spread.1 = f32[8,9,8,384]{3,2,1,0:T(8,128)} custom-call(bf16[4,2,2,16,384]{4,3,2,1,0:T(8,128)(2,1)} %score_users.1.by_slot), custom_call_target="tpu_custom_call" | custom-call | tf_op jit(solution)/shard_map/spread/pallas_call | solution.py:415

commit v5 on v3

--- a/solution.py
+++ b/solution.py
@@ -150,7 +150,7 @@
     def back(o, j):
         s = slot_of(o)
         return pltpu.make_async_remote_copy(
-            results.at[s, sub_at(j)], out.at[s, c], r_send.at[s, j], r_recv.at[s, j],
+            results.at[s, j], out.at[s, c], r_send.at[s, j], r_recv.at[s, j],
             device_id={"blk": partner_of(o), "sub": sub_at(j)},
         )
 
@@ -162,7 +162,7 @@
             device_id={"blk": partner_of(o), "sub": sub_at(j)},
         )
 
-    own_back = pltpu.make_async_copy(results.at[own, c], out.at[own, c], r_send.at[own, 0])
+    own_back = pltpu.make_async_copy(results.at[own, 0], out.at[own, c], r_send.at[own, 0])
 
     for j in range(1, n_x):
         along_x(own, j).start()
@@ -195,16 +195,17 @@
         bias = jnp.where(row == t, bias_task[t], bias)
     user = lax.rem(lax.broadcasted_iota(jnp.int32, (n_hid, n_x * rows), 1) // held, count)
 
-    for j in range(1, n_sub):
-        from_sub(j).wait_recv()
-    for j in range(n_sub):
-        queries[:, j * n_items : (j + 1) * n_items] = projected[j, :width, :]
-        terms[:, j * n_items : (j + 1) * n_items] = projected[j, width:, :].astype(F32)
+    def take_items(j):
+        at = slice(j * n_items, (j + 1) * n_items)
+        queries[:, at] = projected[sub_at(j), :width, :]
+        terms[:, at] = projected[sub_at(j), width:, :].astype(F32)
+
+    take_items(0)
 
     factor = math.log2(math.e) / math.sqrt(width)
     lanes = 256 if all_items % 256 == 0 else 128
 
-    def score(s):
+    def score(s, between):
         block = tokens[s].reshape(n_x * rows, width)
         keys = mm(block, w_key[...]).astype(BF16)
         values = mm(block, w_value[...]).astype(BF16)
@@ -219,6 +220,7 @@
             return jnp.concatenate([array[i : i + held] for i in at], 0)
 
         for low in range(0, all_items, lanes):
+            between(low)
             all_scores = mm(keys, queries[:, low : low + lanes])
             weights = []
             for u in range(count):
@@ -239,20 +241,37 @@
                 j, at = divmod(low + i, n_items)
                 results[s, j, :, at : at + 128] = (logits[:, i : i + 128] + bias).astype(BF16)
 
+    def hand_on(step):
+        later = offset_at(step)
+        from_blk(later).wait_recv()
+        for j in range(1, n_x):
+            along_x(slot_of(later), j).start()
+
+    if n_slots > 1:
+        hand_on(1)
+
     def one_step(step, carry):
         o = offset_at(step)
         s = slot_of(o)
 
-        @pl.when(step + 1 < n_slots)
-        def _():
-            later = offset_at(step + 1)
-            from_blk(later).wait_recv()
-            for j in range(1, n_x):
-                along_x(slot_of(later), j).start()
+        def between(low):
+            if low < n_items < low + lanes or low == n_items:
+
+                @pl.when(step == 0)
+                def _():
+                    for j in range(1, n_sub):
+                        from_sub(j).wait_recv()
+                        take_items(j)
+
+            if low + lanes == all_items:
+
+                @pl.when(step + 2 < n_slots)
+                def _():
+                    hand_on(step + 2)
 
         for j in range(1, n_x):
             from_x(s, j).wait_recv()
-        score(s)
+        score(s, between)
         for j in range(1, n_sub):
             back(o, j).start()
 

time: 27.6 us -> 28.1 us (1.018)
  Pallas kernels: 27.4 us -> 27.9 us
    pallas_call x1, Pallas kernels: 25.6 us -> 26.1 us  [shards(): pl.pallas_call(functools.partial(kernel, n_blk, n_x, n_sub), out_shape=ja...]
where the time goes in v5:
time: 28.1 us; the launch traced here: 27.9 us
  Pallas kernels  27.9 us (99%)
    pallas_call x1, Pallas kernels, shards(): pl.pallas_call(functools.partial(kernel, n_blk, n_x, n_sub), out_shape=ja...  26.1 us
    pallas_call x1, Pallas kernels, shards(): pl.pallas_call(functools.partial(spread, place_of), out_shape=jax.ShapeDt...  1.82 us

profile of v5, /device:TPU:0, one launch (start us, length us, event | category | flops | bytes accessed | tf_op | source)
XLA Modules:
  0.0 27.9 jit_solution(1256031375679568401)
XLA Ops:
  0.0 26.1 %score_users.1.by_slot = bf16[4,2,32,384]{3,2,1,0:T(8,128)(2,1)} custom-call(s32[8]{0:T(128)} %lens.1, f32[8]{0:T(128)} %bias_task.1, bf16[256,256]{1,0:T(8,128)(2,1)} %bitcast.3, bf16[384,512]{1,0:T(8,128)(2,1)} %rest_0_.1, bf16[512,256]{1,0:T(8,128)(2,1)} %rest_1_.1, bf16[512,256]{1,0:T(8,128)(2,1)} %rest_2_.1, bf16[256,128]{1,0:T(8,128)(2,1)} %rest_3_.1, ...), custom_call_target="tpu_custom_call" | custom-call | tf_op jit(solution)/shard_map/score_users/pallas_call | solution.py:338
  26.1 1.8 %spread.1 = f32[8,9,8,384]{3,2,1,0:T(8,128)} custom-call(bf16[4,2,32,384]{3,2,1,0:T(8,128)(2,1)} %score_users.1.by_slot), custom_call_target="tpu_custom_call" | custom-call | tf_op jit(solution)/shard_map/spread/pallas_call | solution.py:366

commit v6 on v4

--- a/solution.py
+++ b/solution.py
@@ -57,8 +57,9 @@
     width = hist.shape[1]
     rows = tokens.shape[3]
     n_task, n_hid = w_task.shape
-    count = results.shape[3] // n_task
+    count = results.shape[2] // n_task // PAIRS
     held = rows // count
+    all_users = PAIRS * count
     n_items = items.shape[0]
     all_items = n_sub * n_items
     me, x, c = lax.axis_index("blk"), lax.axis_index("users"), lax.axis_index("sub")
@@ -70,6 +71,14 @@
                 here = (step == i) if ring else (me == m) & (step == i)
                 o, q = jnp.where(here, entry[0], o), jnp.where(here, entry[1], q)
         return o, q
+
+    def offset_at(step):
+        found = jnp.int32(0)
+        for m in range(1 if ring else n_blk):
+            for i, o in enumerate([o for o, q in table[m] if q == 0]):
+                here = (step == i) if ring else (me == m) & (step == i)
+                found = jnp.where(here, o, found)
+        return found
 
     def slot_of(o):
         return o + lowest
@@ -206,25 +215,22 @@
             there, there, c_send.at[j], c_recv.at[j], device_id={"sub": sub_at(j)}
         )
 
-    def back(o, q, j):
+    def back(o, j):
         s = slot_of(o)
         return pltpu.make_async_remote_copy(
-            results.at[s, q, sub_at(j)], out.at[s, c, q], r_send.at[s, q, j], r_recv.at[s, q, j],
+            results.at[s, j], out.at[s, c], r_send.at[s, j], r_recv.at[s, j],
             device_id={"blk": partner_of(o), "sub": sub_at(j)},
         )
 
-    def from_back(o, q, j):
+    def from_back(o, j):
         s = slot_of(o)
-        there = out.at[s, sub_at(-j), q]
-        return pltpu.make_async_remote_copy(
-            there, there, r_send.at[s, q, j], r_recv.at[s, q, j],
+        there = out.at[s, sub_at(-j)]
+        return pltpu.make_async_remote_copy(
+            there, there, r_send.at[s, j], r_recv.at[s, j],
             device_id={"blk": partner_of(o), "sub": sub_at(j)},
         )
 
-    def own_back(q):
-        return pltpu.make_async_copy(
-            results.at[own, q, c], out.at[own, c, q], r_send.at[own, q, 0]
-        )
+    own_back = pltpu.make_async_copy(results.at[own, 0], out.at[own, c], r_send.at[own, 0])
 
     for q in range(PAIRS):
         for sign in (1, -1):
@@ -241,99 +247,121 @@
     for j in range(1, n_sub):
         along_sub(j).start()
 
-    for step in range(PAIRS, min(n_steps, PAIRS + 2)):
-        hand_on(step)
-
     for copy in loads[5:]:
         copy.wait()
     head = w_task[...].astype(F32)
     nothing = jnp.zeros_like(head)
     heads = jnp.concatenate(
         [
-            jnp.concatenate([head if v == u else nothing for v in range(count)], 1)
-            for u in range(count)
+            jnp.concatenate([head if v == u else nothing for v in range(all_users)], 1)
+            for u in range(all_users)
         ],
         0,
     ).astype(BF16)
-    row = lax.rem(lax.broadcasted_iota(jnp.int32, (count * n_task, 128), 0), n_task)
-    bias = jnp.zeros((count * n_task, 128), F32)
+    row = lax.rem(lax.broadcasted_iota(jnp.int32, (all_users * n_task, 128), 0), n_task)
+    bias = jnp.zeros((all_users * n_task, 128), F32)
     for t in range(n_task):
         bias = jnp.where(row == t, bias_task[t], bias)
-    user = lax.rem(lax.broadcasted_iota(jnp.int32, (n_hid, n_x * rows), 1) // held, count)
-
-    for j in range(1, n_sub):
-        from_sub(j).wait_recv()
-    for j in range(n_sub):
-        queries[:, j * n_items : (j + 1) * n_items] = projected[j, :width, :]
-        terms[:, j * n_items : (j + 1) * n_items] = projected[j, width:, :].astype(F32)
+    token = lax.broadcasted_iota(jnp.int32, (n_hid, PAIRS * n_x * rows), 1)
+    user = token // (n_x * rows) * count + lax.rem(token // held, count)
+
+    def take_items(j):
+        at = slice(j * n_items, (j + 1) * n_items)
+        queries[:, at] = projected[sub_at(j), :width, :]
+        terms[:, at] = projected[sub_at(j), width:, :].astype(F32)
+
+    take_items(0)
+    for step in range(PAIRS, min(n_steps, PAIRS + 2)):
+        hand_on(step)
 
     factor = math.log2(math.e) / math.sqrt(width)
     lanes = 256 if all_items % 256 == 0 else 128
 
-    def score(s, q):
-        block = tokens[s, q].reshape(n_x * rows, width)
+    def score(s, between):
+        block = tokens[s].reshape(PAIRS * n_x * rows, width)
         keys = mm(block, w_key[...]).astype(BF16)
         values = mm(block, w_value[...]).astype(BF16)
         pooled_values = mm(values, w_pooled[...]).T
         by_user = jnp.concatenate(
-            [jnp.where(user == u, pooled_values, 0.0).astype(BF16) for u in range(count)], 0
+            [jnp.where(user == u, pooled_values, 0.0).astype(BF16) for u in range(all_users)], 0
         )
         left_out = jnp.where(block[:, :128].astype(F32) > LEFT_OUT / 2, -jnp.inf, 0.0)
 
         def pieces(array, u):
-            at = [p * rows + u * held for p in range(n_x)]
+            q, v = divmod(u, count)
+            at = [(q * n_x + p) * rows + v * held for p in range(n_x)]
             return jnp.concatenate([array[i : i + held] for i in at], 0)
 
         for low in range(0, all_items, lanes):
+            between(low)
             all_scores = mm(keys, queries[:, low : low + lanes])
             weights = []
-            for u in range(count):
+            for u in range(all_users):
                 scores = pieces(all_scores, u) + jnp.concatenate(
                     [pieces(left_out, u)] * (lanes // 128), 1
                 )
                 expo = jnp.exp2((scores - jnp.max(scores, 0, keepdims=True)) * factor)
                 weights.append((expo * (1.0 / jnp.sum(expo, 0, keepdims=True))).astype(BF16))
             weights = jnp.concatenate(
-                [w[p * held : (p + 1) * held] for p in range(n_x) for w in weights], 0
+                [
+                    w[p * held : (p + 1) * held]
+                    for q in range(PAIRS)
+                    for p in range(n_x)
+                    for w in weights[q * count : (q + 1) * count]
+                ],
+                0,
             )
             layer = mm(by_user, weights) + jnp.concatenate(
-                [terms[:, low : low + lanes]] * count, 0
+                [terms[:, low : low + lanes]] * all_users, 0
             )
             hidden = jnp.maximum(layer.astype(BF16), jnp.zeros((), BF16))
             logits = mm(heads, hidden)
             for i in range(0, lanes, 128):
                 j, at = divmod(low + i, n_items)
-                results[s, q, j, :, at : at + 128] = (logits[:, i : i + 128] + bias).astype(BF16)
+                results[s, j, :, at : at + 128] = (logits[:, i : i + 128] + bias).astype(BF16)
 
     def one_step(step, carry):
-        o, q = step_at(step)
+        o = offset_at(step)
         s = slot_of(o)
-        ahead = jnp.where(step < 2, step + PAIRS + 2, step + PAIRS + 1)
-
-        @pl.when((step != 2) & (ahead < n_steps))
+
+        def between(low):
+            if low < n_items < low + lanes or low == n_items:
+
+                @pl.when(step == 0)
+                def _():
+                    for j in range(1, n_sub):
+                        from_sub(j).wait_recv()
+                        take_items(j)
+
+            for i in range(2):
+                if low == (all_items // lanes - 2 + i) * lanes:
+                    piece = PAIRS + 2 + 2 * step + i
+
+                    @pl.when(piece < n_steps)
+                    def _():
+                        hand_on(piece)
+
+        for q in range(PAIRS):
+            for j in range(1, n_x):
+                from_x(s, q, j).wait_recv()
+        score(s, between)
+        for j in range(1, n_sub):
+            back(o, j).start()
+
+        @pl.when(step == 0)
         def _():
-            hand_on(ahead)
-
-        for j in range(1, n_x):
-            from_x(s, q, j).wait_recv()
-        score(s, q)
-        for j in range(1, n_sub):
-            back(o, q, j).start()
-
-        @pl.when(step < PAIRS)
+            own_back.start()
+
+        @pl.when(step > 0)
         def _():
-            own_back(q).start()
-
-        @pl.when(step >= PAIRS)
-        def _():
-            back(o, q, 0).start()
+            back(o, 0).start()
 
         return carry
 
-    lax.fori_loop(0, n_steps, one_step, jnp.int32(0))
-
+    lax.fori_loop(0, n_slots, one_step, jnp.int32(0))
+
+    own_back.wait()
     for q in range(PAIRS):
-        own_back(q).wait()
         for sign in (1, -1):
             own_along_blk(sign, q, wait_send)
     for step in range(n_steps):
@@ -342,12 +370,12 @@
             relay(o, q, wait_send)
         for j in range(1, n_x):
             along_x(slot_of(o), q, j).wait_send()
-        for j in range(0 if step >= PAIRS else 1, n_sub):
-            back(o, q, j).wait_send()
+    for step in range(n_slots):
+        for j in range(0 if step > 0 else 1, n_sub):
+            back(offset_at(step), j).wait_send()
     for s in range(n_slots):
-        for q in range(PAIRS):
-            for j in range(0 if s != own else 1, n_sub):
-                from_back(s - lowest, q, j).wait_recv()
+        for j in range(0 if s != own else 1, n_sub):
+            from_back(s - lowest, j).wait_recv()
     for j in range(1, n_sub):
         along_sub(j).wait_send()
 
@@ -385,7 +413,7 @@
     )
     by_slot = pl.pallas_call(
         functools.partial(kernel, n_blk, n_x, n_sub),
-        out_shape=jax.ShapeDtypeStruct((n_slots, n_sub, PAIRS, count * n_task, n_items), BF16),
+        out_shape=jax.ShapeDtypeStruct((n_slots, n_sub, PAIRS * count * n_task, n_items), BF16),
         in_specs=[smem, smem, hbm] + [hbm] * len(held_here),
         out_specs=pl.BlockSpec(memory_space=pl.ANY),
         scratch_shapes=[
@@ -394,7 +422,7 @@
             pltpu.VMEM((n_sub, width + n_hid, n_items), BF16),
             pltpu.VMEM((width, n_sub * n_items), BF16),
             pltpu.VMEM((n_hid, n_sub * n_items), F32),
-            pltpu.VMEM((n_slots, PAIRS, n_sub, count * n_task, n_items), BF16),
+            pltpu.VMEM((n_slots, n_sub, PAIRS * count * n_task, n_items), BF16),
             dma((2, PAIRS)),
             dma((n_slots, PAIRS)),
             dma((n_slots, PAIRS)),
@@ -402,8 +430,8 @@
             dma((n_slots, PAIRS, n_x)),
             dma((n_sub,)),
             dma((n_sub,)),
-            dma((n_slots, PAIRS, n_sub)),
-            dma((n_slots, PAIRS, n_sub)),
+            dma((n_slots, n_sub)),
+            dma((n_slots, n_sub)),
             dma((len(held_here),)),
             dma((PAIRS,)),
         ],

time: 29.7 us -> 29 us (0.976)
  Pallas kernels: 29.5 us -> 28.8 us
    pallas_call x1, Pallas kernels: 27.7 us -> 27 us  [shards(): pl.pallas_call(functools.partial(kernel, n_blk, n_x, n_sub), out_shape=ja...]
where the time goes in v6:
time: 29 us; the launch traced here: 28.8 us
  Pallas kernels  28.8 us (99%)
    pallas_call x1, Pallas kernels, shards(): pl.pallas_call(functools.partial(kernel, n_blk, n_x, n_sub), out_shape=ja...  27 us
    pallas_call x1, Pallas kernels, shards(): pl.pallas_call(functools.partial(spread, place_of), out_shape=jax.ShapeDt...  1.82 us

profile of v6, /device:TPU:0, one launch (start us, length us, event | category | flops | bytes accessed | tf_op | source)
XLA Modules:
  0.0 28.8 jit_solution(5109006509003398761)
XLA Ops:
  0.0 27.0 %score_users.1.by_slot = bf16[4,2,32,384]{3,2,1,0:T(8,128)(2,1)} custom-call(s32[8]{0:T(128)} %lens.1, f32[8]{0:T(128)} %bias_task.1, bf16[256,256]{1,0:T(8,128)(2,1)} %bitcast.3, bf16[384,512]{1,0:T(8,128)(2,1)} %rest_0_.1, bf16[512,256]{1,0:T(8,128)(2,1)} %rest_1_.1, bf16[512,256]{1,0:T(8,128)(2,1)} %rest_2_.1, bf16[256,128]{1,0:T(8,128)(2,1)} %rest_3_.1, ...), custom_call_target="tpu_custom_call" | custom-call | tf_op jit(solution)/shard_map/score_users/pallas_call | solution.py:414
  27.0 1.8 %spread.1 = f32[8,9,8,384]{3,2,1,0:T(8,128)} custom-call(bf16[4,2,32,384]{3,2,1,0:T(8,128)(2,1)} %score_users.1.by_slot), custom_call_target="tpu_custom_call" | custom-call | tf_op jit(solution)/shard_map/spread/pallas_call | solution.py:443

commit v7 on v3

--- a/solution.py
+++ b/solution.py
@@ -27,10 +27,10 @@
 
 def partner_offsets(n_blk):
     if n_blk >= WIN:
-        near = [0] + [sign * d for d in range(1, REACH + 1) for sign in (1, -1)]
+        near = [0] + [sign * d for d in range(REACH, 0, -1) for sign in (1, -1)]
         return [near] * n_blk
     return [
-        [(m - g) % n_blk for g in sorted(range(n_blk), key=lambda g: (abs(g - m), g))]
+        [(m - g) % n_blk for g in sorted(range(n_blk), key=lambda g: (g != m, -abs(g - m), g))]
         for m in range(n_blk)
     ]
 

time: 27.6 us -> 25.5 us (0.924)
  Pallas kernels: 27.4 us -> 25.3 us
    pallas_call x1, Pallas kernels: 25.6 us -> 23.5 us  [shards(): pl.pallas_call(functools.partial(kernel, n_blk, n_x, n_sub), out_shape=ja...]
where the time goes in v7:
time: 25.5 us; the launch traced here: 25.3 us
  Pallas kernels  25.3 us (99%)
    pallas_call x1, Pallas kernels, shards(): pl.pallas_call(functools.partial(kernel, n_blk, n_x, n_sub), out_shape=ja...  23.5 us
    pallas_call x1, Pallas kernels, shards(): pl.pallas_call(functools.partial(spread, place_of), out_shape=jax.ShapeDt...  1.82 us

profile of v7, /device:TPU:0, one launch (start us, length us, event | category | flops | bytes accessed | tf_op | source)
XLA Modules:
  0.0 25.3 jit_solution(5627625238707308805)
XLA Ops:
  0.0 23.5 %score_users.1.by_slot = bf16[4,2,32,384]{3,2,1,0:T(8,128)(2,1)} custom-call(s32[8]{0:T(128)} %lens.1, f32[8]{0:T(128)} %bias_task.1, bf16[256,256]{1,0:T(8,128)(2,1)} %bitcast.3, bf16[384,512]{1,0:T(8,128)(2,1)} %rest_0_.1, bf16[512,256]{1,0:T(8,128)(2,1)} %rest_1_.1, bf16[512,256]{1,0:T(8,128)(2,1)} %rest_2_.1, bf16[256,128]{1,0:T(8,128)(2,1)} %rest_3_.1, ...), custom_call_target="tpu_custom_call" | custom-call | tf_op jit(solution)/shard_map/score_users/pallas_call | solution.py:319
  23.5 1.8 %spread.1 = f32[8,9,8,384]{3,2,1,0:T(8,128)} custom-call(bf16[4,2,32,384]{3,2,1,0:T(8,128)(2,1)} %score_users.1.by_slot), custom_call_target="tpu_custom_call" | custom-call | tf_op jit(solution)/shard_map/spread/pallas_call | solution.py:347
